TPU v7x, 32 devices: a whole 2x2x4 slice. The times are simulated.
32 devices in a mesh: seq: 4 (over z), tensor: 8 (over y, x, core).
Axes of the slice: x: 2, y: 2, z: 4, core: 2. Of those that a mesh axis runs over, the one named last changes fastest.
Arguments:
- layer_inputs: bfloat16 [768, 6144], P('seq'), may hold values from -16 to 16
- projection_matrices: bfloat16 [6144, 3, 768], P(None, None, 'tensor'), may hold values from -0.109375 to 0.109375
- result_sensitivity: bfloat16 [768, 768], P('seq', 'tensor'), may hold values from -4.5 to 4.5
- channel_fading_rate: float32 [8], P('tensor'), may hold values from 2.6041667e-05 to 0.03
- loss_events: int32 [4], replicated, may hold values from 0 to 767
Outputs:
- input_grad: bfloat16 [6144, 768], P('tensor', 'seq')
- weight_grad: bfloat16 [6144, 3, 768], P('seq', None, 'tensor')
All inputs are finite; a program needn't handle non-finite values.
Results may differ from a plain program's by a relative error of at most 0.023.
Values may be sent and summed in bfloat16 or wider, within the bound.
A program may use at most 64 MiB of HBM per device.

v0:
```python
import math

import jax
import jax.numpy as jnp
from jax import lax
from jax.sharding import PartitionSpec as P

DH = 96


DROP_LOGARITHM = 0.3
CLIP_RMS = 0.5
EXACT = lax.Precision.HIGHEST


def body(layer_inputs, projection_matrices, result_sensitivity, channel_fading_rate, loss_events):
    row_count = layer_inputs.shape[0]
    head_count = result_sensitivity.shape[1] // DH
    scale = DH ** (-0.5)
    proj = jnp.einsum(
        "td,dpe->pte", layer_inputs, projection_matrices, preferred_element_type=jnp.float32
    )

    def per_head(flat):
        return flat.reshape(row_count, head_count, DH).transpose(1, 0, 2).astype(jnp.float32)

    query = per_head((proj[0] * scale).astype(jnp.bfloat16))
    keys = per_head(proj[1].astype(jnp.bfloat16))
    values = per_head(proj[2].astype(jnp.bfloat16))
    grads_out = per_head(result_sensitivity)
    element_location = lax.axis_index("seq") * row_count + jnp.arange(row_count, dtype=jnp.int32)
    memory_loss_sites = jnp.sum(
        (loss_events[None, :] == element_location[:, None]).astype(jnp.float32), axis=1
    )
    logarithm_values = -(channel_fading_rate[:, None] + DROP_LOGARITHM * memory_loss_sites[None, :])
    cumul = jnp.cumsum(logarithm_values, axis=1)
    totals = cumul[:, -1]
    tail_w = jnp.exp(totals[:, None] - cumul)
    head_w = jnp.exp(cumul)
    fwd_state = jnp.einsum("nsf,nse->nfe", values * tail_w[..., None], keys, precision=EXACT)
    rev_state = jnp.einsum("nte,ntf->nef", query * head_w[..., None], grads_out, precision=EXACT)
    all_tot, all_fwd, all_rev = (
        lax.all_gather(totals[None].astype(jnp.bfloat16), "seq", axis=0, tiled=True).astype(
            jnp.float32
        ),
        lax.all_gather(fwd_state[None].astype(jnp.bfloat16), "seq", axis=0, tiled=True).astype(
            jnp.float32
        ),
        lax.all_gather(rev_state[None].astype(jnp.bfloat16), "seq", axis=0, tiled=True).astype(
            jnp.float32
        ),
    )
    index = lax.axis_index("seq")
    ends = jnp.cumsum(all_tot, axis=0)
    bases = ends - all_tot
    mine_end = lax.dynamic_index_in_dim(ends, index, 0, keepdims=False)
    mine_base = lax.dynamic_index_in_dim(bases, index, 0, keepdims=False)
    order = jnp.arange(all_tot.shape[0], dtype=jnp.int32)
    before = (order < index)[:, None]
    after = (order > index)[:, None]
    fwd_w = jnp.exp(jnp.where(before, mine_base[None, :] - ends, -jnp.inf))
    rev_w = jnp.exp(jnp.where(after, bases - mine_end[None, :], -jnp.inf))
    prefix = jnp.einsum("jn,jnfe->nfe", fwd_w, all_fwd, precision=EXACT)
    suffix = jnp.einsum("jn,jnef->nef", rev_w, all_rev, precision=EXACT)
    steps_idx = jnp.arange(row_count)
    later = (steps_idx[:, None] >= steps_idx[None, :])[None]
    weight = jnp.exp(jnp.where(later, cumul[:, :, None] - cumul[:, None, :], -jnp.inf))
    scores = jnp.einsum("nte,nse->nts", query, keys, precision=EXACT) * weight
    dscores = jnp.einsum("ntf,nsf->nts", grads_out, values, precision=EXACT) * weight
    dquery = jnp.einsum("nts,nse->nte", dscores, keys, precision=EXACT) + head_w[
        ..., None
    ] * jnp.einsum("ntf,nfe->nte", grads_out, prefix, precision=EXACT)
    dkey = jnp.einsum("nts,nte->nse", dscores, query, precision=EXACT) + tail_w[
        ..., None
    ] * jnp.einsum("nsf,nef->nse", values, suffix, precision=EXACT)
    dvalue = jnp.einsum("nts,ntf->nsf", scores, grads_out, precision=EXACT) + tail_w[
        ..., None
    ] * jnp.einsum("nse,nef->nsf", keys, suffix, precision=EXACT)
    stacked = jnp.stack([dquery * scale, dkey, dvalue]).astype(jnp.bfloat16)
    grads = stacked.transpose(0, 2, 1, 3).reshape(3, row_count, head_count * DH)
    piece = projection_matrices
    input_sum = lax.psum_scatter(
        jnp.einsum("rpe,pte->rt", piece, grads, preferred_element_type=jnp.float32),
        "tensor",
        scatter_dimension=0,
        tiled=True,
    )
    piece = layer_inputs
    summed = lax.psum_scatter(
        jnp.einsum("tr,pte->rpe", piece, grads, preferred_element_type=jnp.float32).astype(
            jnp.bfloat16
        ),
        "seq",
        scatter_dimension=0,
        tiled=True,
    ).astype(jnp.float32)
    square = lax.psum(jnp.sum(summed * summed), ("seq", "tensor"))
    entries = layer_inputs.shape[1] * 3 * head_count * DH * lax.axis_size("tensor")
    factor = jnp.minimum(1.0, CLIP_RMS * math.sqrt(entries) / jnp.sqrt(square + 1e-06))
    return (input_sum.astype(jnp.bfloat16), (summed * factor).astype(jnp.bfloat16))


def solution(mesh):
    return jax.shard_map(
        body,
        mesh=mesh,
        in_specs=(P("seq", None), P(None, None, "tensor"), P("seq", "tensor"), P("tensor"), P()),
        out_specs=(P("tensor", "seq"), P("seq", None, "tensor")),
        check_vma=False,
    )
```

profile of v0, /device:TPU:0, one launch (start us, length us, event | category | flops | bytes accessed | tf_op | source)
XLA Modules:
  0.0 209.6 jit_solution(11196409476438257856)
XLA Ops:
  8.0 0.9 convert_reduce_fusion
  9.8 0.6 slice.34
  11.0 0.7 subtract_exponential_fusion
  11.7 2.8 %fusion.63 = (bf16[3,192,96]{1,2,0:T(8,128)(2,1)S(1)}, f32[3,192,96]{1,2,0:T(8,128)S(1)}) fusion(bf16[6144,3,96]{0,2,1:T(8,128)(2,1)S(1)} %copy-done, bf16[192,6144]{1,0:T(8,128)(2,1)} %param.5), kind=kOutput, calls=%fused_computation.84 | convolution fusion | flops 679532544 | bytes 6230016 | tf_op jit(solution)/shard_map/td,dpe->pte/dot_general | solution.py:20
  15.0 0.9 fusion.33
  15.8 1.0 fusion.42
  16.8 0.9 fusion.64
  17.7 0.8 convolution_convert_fusion.1
  18.5 0.6 dynamic-slice
  19.1 0.7 dynamic-update-slice
  19.9 16.7 %all-gather.1 = bf16[384,96]{1,0:T(8,128)(2,1)} all-gather(bf16[96,96]{1,0:T(8,128)(2,1)} %convolution_convert_fusion.1), channel_id=3, replica_groups=mesh['seq'=4,'tensor'=8] {'seq'}, dimensions={0}, use_global_device_ids=true | all-gather | bytes 92160 | tf_op jit(solution)/shard_map/all_gather | solution.py:49
  36.6 10.8 %all-reduce.1 = bf16[4]{0:T(256)(128)(2,1)S(1)} all-reduce(bf16[4]{0:T(256)(128)(2,1)S(1)} %dynamic-update-slice), channel_id=1, replica_groups=mesh['seq'=4,'tensor'=8] {'seq'}, use_global_device_ids=true, to_apply=%add.1 | all-reduce | flops 4 | bytes 16
  47.5 0.5 copy-done.7
  48.1 0.6 fusion.59
  48.7 0.7 constant_dynamic-slice_fusion
  49.4 1.0 convolution_convert_fusion.2
  50.4 0.6 constant_dynamic-slice_fusion.1
  50.9 1.9 fusion.28
  52.8 1.2 fusion.18
  54.1 1.2 fusion.19
  55.3 13.3 %all-gather = bf16[384,96]{1,0:T(8,128)(2,1)S(1)} all-gather(bf16[96,96]{1,0:T(8,128)(2,1)S(1)} %convolution_convert_fusion.2), channel_id=2, replica_groups=mesh['seq'=4,'tensor'=8] {'seq'}, dimensions={0}, use_global_device_ids=true | all-gather | bytes 92160 | tf_op jit(solution)/shard_map/all_gather | solution.py:46
  68.6 0.9 fusion.30
  69.4 1.1 fusion.20
  70.6 0.6 copy-done.3
  71.2 4.5 %fusion = bf16[6144,3,96]{0,2,1:T(8,128)(2,1)} fusion(bf16[192,6144]{1,0:T(8,128)(2,1)} %param.5, bf16[1,192,96]{2,1,0:T(8,128)(2,1)S(1)} %fusion.18, bf16[1,192,96]{2,1,0:T(8,128)(2,1)S(1)} %fusion.19, bf16[1,192,96]{2,1,0:T(8,128)(2,1)S(1)} %fusion.20), kind=kOutput, calls=%fused_computation.2 | convolution fusion | flops 681357312 | bytes 6008832 | tf_op jit(solution)/shard_map/tr,pte->rpe/dot_general | solution.py:90
  75.8 4.4 %convolution_bitcast_fusion = f32[6144,192]{0,1:T(8,128)} fusion(bf16[6144,3,96]{0,2,1:T(8,128)(2,1)S(1)} %copy-done, bf16[1,192,96]{2,1,0:T(8,128)(2,1)} %copy-done.1, bf16[1,192,96]{2,1,0:T(8,128)(2,1)} %copy-done.2, bf16[1,192,96]{2,1,0:T(8,128)(2,1)} %copy-done.3), kind=kOutput, calls=%fused_computation.1 | convolution fusion | flops 679587840 | bytes 8368128 | tf_op jit(solution)/shard_map/rpe,pte->rt/dot_general | solution.py:83
  80.2 60.3 %reduce-scatter.5.cloned.1.call-done = bf16[1536,3,96]{0,2,1:T(8,128)(2,1)} async-done(((bf16[6144,3,96]{0,2,1:T(8,128)(2,1)}), bf16[1536,3,96]{0,2,1:T(8,128)(2,1)}) %reduce-scatter.5.cloned.1.call-update) | async-done | bytes 884752 | tf_op jit(solution)/shard_map/reduce_scatter | solution.py:89
  140.5 2.2 %fusion.4 = f32[]{:T(128)} fusion(bf16[1536,3,96]{0,2,1:T(8,128)(2,1)} %reduce-scatter.5.cloned.1.call-done), kind=kLoop, calls=%fused_computation.8 | loop fusion | flops 1327103 | bytes 884740 | tf_op jit(solution)/shard_map/reduce_sum | solution.py:97
  142.7 40.9 %psum.7 = f32[]{:T(128)} all-reduce(f32[]{:T(128)} %fusion.4), channel_id=1, replica_groups=mesh['seq'=4,'tensor'=8] {'seq','tensor'}, use_global_device_ids=true, to_apply=%region_7.8 | all-reduce | flops 1 | bytes 8 | tf_op jit(solution)/shard_map/psum | solution.py:97
  184.3 14.5 %reduce-scatter.3.cloned.1.call-done = f32[768,192]{0,1:T(8,128)} async-done(((f32[6144,192]{0,1:T(8,128)}), f32[768,192]{0,1:T(8,128)}) %reduce-scatter.3.cloned.1.call-update) | async-done | bytes 589840 | tf_op jit(solution)/shard_map/reduce_scatter | solution.py:82
  198.8 1.8 convert_element_type.74
  200.6 2.2 %fusion.5 = bf16[1536,3,96]{0,2,1:T(8,128)(2,1)} fusion(bf16[1536,3,96]{0,2,1:T(8,128)(2,1)} %reduce-scatter.5.cloned.1.call-done, f32[]{:T(128)S(6)} %min_shard_map.3), kind=kLoop, calls=%fused_computation.9 | loop fusion | flops 1327104 | bytes 1769476 | tf_op jit(solution)/shard_map/convert_element_type | solution.py:100
  (32 shorter events, 1.6 us)
Async XLA Ops:
  7.2 4.5 %copy-start = (bf16[6144,3,96]{0,2,1:T(8,128)(2,1)S(1)}, bf16[6144,3,96]{0,2,1:T(8,128)(2,1)}, u32[]{:S(2)}) copy-start(bf16[6144,3,96]{0,2,1:T(8,128)(2,1)} %param.6) | copy-start | bytes 10616836
  7.2 133.3 %reduce-scatter.5.cloned.1.call-start = ((), (), s32[]{:S(2)}) async-start(), calls=%async_computation.3 | async-start | bytes 4423680 | tf_op jit(solution)/shard_map/reduce_scatter | solution.py:89
  11.7 3.1 %copy-start.4 = (bf16[192,96]{1,0:T(8,128)(2,1)S(1)}, bf16[192,96]{1,0:T(8,128)(2,1)}, u32[]{:S(2)}) copy-start(bf16[192,96]{1,0:T(8,128)(2,1)} %param.7) | copy-start | bytes 110596
  11.7 6.8 %copy-start.6 = (u32[32]{0:T(128)S(1)}, u32[32]{0:T(128)}, u32[]{:S(2)}) copy-start(u32[32]{0:T(128)} %constant.41) | copy-start | bytes 388
  14.5 3.2 %copy-start.5 = (bf16[3,192,96]{1,2,0:T(8,128)(2,1)}, bf16[3,192,96]{1,2,0:T(8,128)(2,1)S(1)}, u32[]{:S(2)}) copy-start(bf16[3,192,96]{1,2,0:T(8,128)(2,1)S(1)} %get-tuple-element.5) | copy-start | bytes 331780
  47.5 0.5 copy-start.7
  54.0 16.5 %copy-start.1 = (bf16[1,192,96]{2,1,0:T(8,128)(2,1)}, bf16[1,192,96]{2,1,0:T(8,128)(2,1)S(1)}, u32[]{:S(2)}) copy-start(bf16[1,192,96]{2,1,0:T(8,128)(2,1)S(1)} %fusion.18) | copy-start | bytes 110596
  55.3 15.3 %copy-start.2 = (bf16[1,192,96]{2,1,0:T(8,128)(2,1)}, bf16[1,192,96]{2,1,0:T(8,128)(2,1)S(1)}, u32[]{:S(2)}) copy-start(bf16[1,192,96]{2,1,0:T(8,128)(2,1)S(1)} %fusion.19) | copy-start | bytes 110596
  70.6 0.6 copy-start.3
  75.8 123.0 %reduce-scatter.3.cloned.1.call-start = ((), (), s32[]{:S(2)}) async-start(), calls=%async_computation.2 | async-start | bytes 5308416 | tf_op jit(solution)/shard_map/reduce_scatter | solution.py:82
Sparse Core Ops, SparseCore 0:
  75.9 64.5 reduce-scatter.4
  143.9 54.7 reduce-scatter.2
where the time goes:
time: 210 us
  blocking collectives  81.8 us (39%)
  waiting for transfers between devices  74.8 us (36%)
  matrix products  23 us (11%)
  between operations  16.4 us (8%)
  other arithmetic  9.12 us (4%)
  local copies, waits for them, and re-layouts  4.56 us (2%)
    reduce_scatter x1, waiting for transfers between devices, body(): lax.psum_scatter(jnp.einsum('tr,pte->rpe', piece, grads, preferred_elemen...  60.3 us
    psum x1, blocking collectives, body(): square = lax.psum(jnp.sum(summed * summed), ('seq', 'tensor'))  40.9 us
    all_gather x1, blocking collectives, body(): lax.all_gather(rev_state[None].astype(jnp.bfloat16), 'seq', axis=0, tiled...  16.7 us
    reduce_scatter x1, waiting for transfers between devices, body(): lax.psum_scatter(jnp.einsum('rpe,pte->rt', piece, grads, preferred_elemen...  14.5 us
    all_gather x1, blocking collectives, body(): lax.all_gather(fwd_state[None].astype(jnp.bfloat16), 'seq', axis=0, tiled...  13.3 us
    unnamed x1, blocking collectives  10.8 us
    dot_general x1, matrix products, body(): jnp.einsum('tr,pte->rpe', piece, grads, preferred_element_type=jnp.float32)  4.54 us
    dot_general x1, matrix products, body(): jnp.einsum('rpe,pte->rt', piece, grads, preferred_element_type=jnp.float32)  4.42 us
  transfers between devices with their start and end apart: 2, of which 2 were waited for; matrix products, arithmetic and copies ran while one was open for 3% of the time, Pallas kernels for 0%

commit v1 on v0

v1 whole, which is shorter than its diff:
```python
import functools
import math

import jax
import jax.numpy as jnp
from jax import lax
from jax.experimental import pallas as pl
from jax.experimental.pallas import tpu as pltpu
from jax.sharding import PartitionSpec as P

DH = 96
DROP_LOGARITHM = 0.3
CLIP_RMS = 0.5
MESH = pl.DeviceIdType.MESH
F32 = jnp.float32
BF16 = jnp.bfloat16
LOAD_CHUNKS = 4


def mm(a, b):
    return jnp.dot(a, b, preferred_element_type=F32)


def mm_nt(a, b):
    return lax.dot_general(a, b, (((1,), (1,)), ((), ())), preferred_element_type=F32)


def kernel(
    n_seq, n_t, entries, aligned,
    x_hbm, w_hbm, wb_hbm, o_ref, rate_ref, events_ref,
    ig_ref, wg_ref,
    x, w, wb, xg, g, gt, st, ps, rc, sd, rd, acc, sqz, sqt,
    load_sem, bx1s, bx1r, bx2s, bx2r, bx3s, bx3r, sts, str_, gs, gr,
    pss, psr, rds, rdr, zs, zr, ts, tr,
):
    rows, width = x_hbm.shape
    blk = width // n_seq
    iblk = width // n_t
    scale = DH ** (-0.5)
    s = lax.axis_index("seq")
    j = lax.axis_index("tensor")
    nc = n_t // 2
    k = lax.rem(j, 2)
    chip = j // 2
    sibling = j + 1 - 2 * k
    group = (j // 8) * 8
    c = lax.rem(j, 8) // 2
    q = blk // 4
    half = rows // 2

    wide = width // LOAD_CHUNKS
    loads = []
    for i in range(LOAD_CHUNKS):
        cols = pl.ds(i * wide, wide)
        for n, (src, dst) in enumerate(((x_hbm, x), (w_hbm, w))):
            copy = pltpu.make_async_copy(src.at[:, cols], dst.at[:, cols], load_sem.at[2 * i + n])
            copy.start()
            loads.append(copy)
    if not aligned:
        wb_copy = pltpu.make_async_copy(wb_hbm, wb, load_sem.at[2 * LOAD_CHUNKS])
        wb_copy.start()

    def seq_peer(d):
        return lax.rem(s + d, n_seq)

    def t_peer(d):
        return lax.rem(j + d, n_t)

    barrier = pltpu.get_barrier_semaphore()
    for d in range(1, n_seq):
        pl.semaphore_signal(barrier, inc=1, device_id=(seq_peer(d), j), device_id_type=MESH)
    for d in range(1, n_t):
        pl.semaphore_signal(barrier, inc=1, device_id=(s, t_peer(d)), device_id_type=MESH)
    pl.semaphore_wait(barrier, n_seq + n_t - 2)

    sends = []

    def send(src, dst, ssem, rsem, device):
        copy = pltpu.make_async_remote_copy(
            src_ref=src, dst_ref=dst, send_sem=ssem, recv_sem=rsem,
            device_id=device, device_id_type=MESH,
        )
        copy.start()
        sends.append(copy)

    def wait_recv(ref, ssem, rsem, device):
        pltpu.make_async_remote_copy(
            src_ref=ref, dst_ref=ref, send_sem=ssem, recv_sem=rsem,
            device_id=device, device_id_type=MESH,
        ).wait_recv()

    def piece(d, core, chip_col):
        return xg.at[
            d - 1,
            pl.ds(pl.multiple_of(core * half, 32), half),
            pl.ds(pl.multiple_of(chip_col * q, 128), q),
        ]

    def token_half(d, core):
        return xg.at[d - 1, pl.ds(pl.multiple_of(core * half, 32), half), :]

    for d in range(1, n_seq):
        src = x_hbm.at[
            pl.ds(pl.multiple_of(k * half, 32), half),
            pl.ds(pl.multiple_of(seq_peer(d) * blk + c * q, 128), q),
        ]
        send(src, piece(d, k, c), bx1s.at[d - 1], bx1r.at[d - 1], (seq_peer(d), j))

    proj = jnp.zeros((3 * DH, rows), F32)
    for i in range(LOAD_CHUNKS):
        cols = pl.ds(i * wide, wide)
        loads[2 * i].wait()
        loads[2 * i + 1].wait()
        proj = proj + mm_nt(w[:, cols], x[:, cols])
    q_t = (proj[:DH] * scale).astype(BF16)
    k_t = proj[DH : 2 * DH].astype(BF16)
    v_t = proj[2 * DH :].astype(BF16)
    o = o_ref[...]
    o_t = o.astype(F32).T.astype(BF16)
    q_r = q_t.astype(F32).T.astype(BF16)
    v_r = v_t.astype(F32).T.astype(BF16)

    rate = rate_ref[0]
    n_events = events_ref.shape[0]
    base = s * rows
    lane = lax.broadcasted_iota(jnp.int32, (1, rows), 1)

    def events_in(low, high):
        total = jnp.zeros(jnp.broadcast_shapes(jnp.shape(low), jnp.shape(high)), F32)
        for n in range(n_events):
            e = events_ref[n]
            total = total + jnp.where((e > low) & (e <= high), 1.0, 0.0)
        return total

    last = jnp.full((1, rows), rows - 1, jnp.int32) + base
    before = jnp.full((1, rows), -1, jnp.int32) + base
    here = lane + base
    head_w = jnp.exp(-(rate * (lane + 1).astype(F32) + DROP_LOGARITHM * events_in(before, here)))
    tail_w = jnp.exp(
        -(rate * (rows - 1 - lane).astype(F32) + DROP_LOGARITHM * events_in(here, last))
    )

    st[0, 0] = mm((k_t.astype(F32) * tail_w).astype(BF16), v_r).astype(BF16)
    st[1, 0] = mm((q_t.astype(F32) * head_w).astype(BF16), o).astype(BF16)
    for d in range(1, n_seq):
        earlier = jnp.where(seq_peer(d) < s, 1, 0)
        send(st.at[earlier, 0], st.at[0, d], sts.at[d - 1], str_.at[d - 1], (seq_peer(d), j))

    for d in range(1, n_seq):
        wait_recv(piece(d, k, c), bx1s.at[d - 1], bx1r.at[d - 1], (s, j))
        for m in range(1, 4):
            to = group + 2 * lax.rem(c + m, 4) + k
            mine = piece(d, k, c)
            send(mine, mine, bx2s.at[d - 1, m - 1], bx2r.at[d - 1, m - 1], (s, to))

    t_idx = lax.broadcasted_iota(jnp.int32, (rows, rows), 0)
    s_idx = lax.broadcasted_iota(jnp.int32, (rows, rows), 1)
    decay = rate * (t_idx - s_idx).astype(F32) + DROP_LOGARITHM * events_in(
        s_idx + base, t_idx + base
    )
    weight = jnp.where(t_idx >= s_idx, jnp.exp(-jnp.maximum(decay, 0.0)), 0.0)
    scores = (mm(q_r, k_t) * weight).astype(BF16)
    dscores = (mm(o, v_t) * weight).astype(BF16)
    dq_t = mm_nt(k_t, dscores)
    dk_t = mm(q_t, dscores)
    dv_t = mm(o_t, scores)

    prefix = jnp.zeros((DH, DH), F32)
    suffix = jnp.zeros((DH, DH), F32)
    zero = jnp.zeros((1, DH), jnp.int32)
    for d in range(1, n_seq):
        wait_recv(st.at[0, d], sts.at[d - 1], str_.at[d - 1], (s, j))
        src = lax.rem(s + n_seq - d, n_seq)
        state = st[0, d].astype(F32)
        low = jnp.minimum(src, s)
        high = jnp.maximum(src, s)
        gap = rate * ((high - low - 1) * rows).astype(F32) + DROP_LOGARITHM * events_in(
            zero + ((low + 1) * rows - 1), zero + (high * rows - 1)
        )
        state = state * jnp.exp(-gap)
        is_fwd = (zero + src) < (zero + s)
        prefix = prefix + jnp.where(is_fwd, state, 0.0)
        suffix = suffix + jnp.where(is_fwd, 0.0, state)
    dq_t = dq_t + mm(prefix.astype(BF16), o_t) * head_w
    dk_t = dk_t + mm(suffix.astype(BF16), v_t) * tail_w
    dv_t = dv_t + mm(suffix.T.astype(BF16), k_t) * tail_w
    grads_t = jnp.concatenate([dq_t * scale, dk_t, dv_t], axis=0)
    gt[0] = grads_t.astype(BF16)
    g[...] = grads_t.T.astype(BF16)
    for d in range(1, n_seq):
        send(gt.at[0], gt.at[d], gs.at[d - 1], gr.at[d - 1], (seq_peer(d), j))

    step = 256 if iblk % 256 == 0 else iblk
    if not aligned:
        wb_copy.wait()

    def block_term(owner, put):
        if aligned:
            def one(i, carry):
                cols = pl.ds(pl.multiple_of(owner * iblk + i * step, 128), step)
                put(pl.ds(pl.multiple_of(i * step, 128), step), mm(g[...], w[:, cols]))
                return carry
            lax.fori_loop(0, iblk // step, one, 0)
        else:
            put(pl.ds(0, iblk), mm(g[...], wb[owner]))

    for m in range(1, nc + 1):
        to_chip = lax.rem(chip + m, nc)
        def put(cols, value, m=m):
            ps[m - 1, :, cols] = value.astype(BF16)
        block_term(2 * to_chip + 1 - k, put)
        send(ps.at[m - 1], rc.at[m - 1], pss.at[m - 1], psr.at[m - 1], (s, sibling))

    for d in range(1, n_seq):
        for m in range(1, 4):
            wait_recv(
                piece(d, k, lax.rem(c + 4 - m, 4)),
                bx2s.at[d - 1, m - 1], bx2r.at[d - 1, m - 1], (s, j),
            )
        send(token_half(d, k), token_half(d, k), bx3s.at[d - 1], bx3r.at[d - 1], (s, sibling))

    for m in range(1, nc):
        wait_recv(rc.at[m - 1], pss.at[m - 1], psr.at[m - 1], (s, sibling))
        to_chip = lax.rem(chip + m, nc)
        def put(cols, value, m=m):
            sd[m - 1, :, cols] = (value + rc[m - 1, :, cols].astype(F32)).astype(BF16)
        block_term(2 * to_chip + k, put)
        send(sd.at[m - 1], rd.at[m - 1], rds.at[m - 1], rdr.at[m - 1], (s, 2 * to_chip + k))

    wstep = 256
    for d in range(1, n_seq):
        wait_recv(token_half(d, 1 - k), bx3s.at[d - 1], bx3r.at[d - 1], (s, sibling))
        wait_recv(gt.at[d], gs.at[d - 1], gr.at[d - 1], (s, j))

    def grad_cols(i, square):
        cols = pl.ds(pl.multiple_of(i * wstep, 128), wstep)
        total = mm(gt[0], x[:, pl.ds(pl.multiple_of(s * blk + i * wstep, 128), wstep)])
        for d in range(1, n_seq):
            total = total + mm(gt[d], xg[d - 1, :, cols])
        acc[:, cols] = total
        return square + jnp.sum((total * total).reshape(3 * DH // 8, 8, wstep), axis=0)

    square = lax.fori_loop(0, blk // wstep, grad_cols, jnp.zeros((8, wstep), F32))
    sqz[0] = square[:, :128] + square[:, 128:]
    for d in range(1, n_seq):
        send(sqz.at[0], sqz.at[d], zs.at[d - 1], zr.at[d - 1], (seq_peer(d), j))

    wait_recv(rc.at[nc - 1], pss.at[nc - 1], psr.at[nc - 1], (s, sibling))
    for m in range(1, nc):
        wait_recv(rd.at[m - 1], rds.at[m - 1], rdr.at[m - 1], (s, j))

    def put(cols, value):
        total = value + rc[nc - 1, :, cols].astype(F32)
        for m in range(1, nc):
            total = total + rd[m - 1, :, cols].astype(F32)
        ig_ref[:, cols] = total.astype(BF16)

    for d in range(1, n_seq):
        wait_recv(sqz.at[d], zs.at[d - 1], zr.at[d - 1], (s, j))
    total = sqz[0]
    for d in range(1, n_seq):
        total = total + sqz[d]
    sqt[0] = total
    for d in range(1, n_t):
        send(sqt.at[0], sqt.at[d], ts.at[d - 1], tr.at[d - 1], (s, t_peer(d)))
    block_term(j, put)
    for d in range(1, n_t):
        wait_recv(sqt.at[d], ts.at[d - 1], tr.at[d - 1], (s, j))
    total = sqt[0]
    for d in range(1, n_t):
        total = total + sqt[d]
    total = jnp.sum(jnp.sum(total, axis=1, keepdims=True), axis=0, keepdims=True)
    factor = jnp.minimum(1.0, CLIP_RMS * math.sqrt(entries) / jnp.sqrt(total + 1e-06))

    def scaled(i, carry):
        cols = pl.ds(pl.multiple_of(i * wstep, 128), wstep)
        wg_ref[:, cols] = (acc[:, cols] * factor).astype(BF16)
        return carry

    lax.fori_loop(0, blk // wstep, scaled, 0)
    for copy in sends:
        copy.wait_send()


def body(n_seq, n_t, layer_inputs, projection_matrices, result_sensitivity, rate, events):
    rows, width = layer_inputs.shape
    blk, iblk, nc = width // n_seq, width // n_t, n_t // 2
    aligned = iblk % 128 == 0
    w_t = projection_matrices.transpose(1, 2, 0).reshape(3 * DH, width)
    if aligned:
        w_b = jnp.zeros((1, 8, 128), BF16)
    else:
        w_b = w_t.reshape(3 * DH, n_t, iblk).transpose(1, 0, 2)
    entries = width * 3 * DH * n_t
    dma = pltpu.SemaphoreType.DMA
    anywhere = pl.BlockSpec(memory_space=pl.ANY)
    vmem = pl.BlockSpec(memory_space=pltpu.VMEM)
    smem = pl.BlockSpec(memory_space=pltpu.SMEM)
    z = n_seq - 1
    input_t, weight_t = pl.pallas_call(
        functools.partial(kernel, n_seq, n_t, entries, aligned),
        out_shape=(
            jax.ShapeDtypeStruct((rows, iblk), BF16),
            jax.ShapeDtypeStruct((3 * DH, blk), BF16),
        ),
        in_specs=[anywhere, anywhere, anywhere, vmem, smem, smem],
        out_specs=(vmem, vmem),
        scratch_shapes=[
            pltpu.VMEM((rows, width), BF16),
            pltpu.VMEM((3 * DH, width), BF16),
            pltpu.VMEM(w_b.shape, BF16),
            pltpu.VMEM((z, rows, blk), BF16),
            pltpu.VMEM((rows, 3 * DH), BF16),
            pltpu.VMEM((n_seq, 3 * DH, rows), BF16),
            pltpu.VMEM((2, n_seq, DH, DH), BF16),
            pltpu.VMEM((nc, rows, iblk), BF16),
            pltpu.VMEM((nc, rows, iblk), BF16),
            pltpu.VMEM((nc - 1, rows, iblk), BF16),
            pltpu.VMEM((nc - 1, rows, iblk), BF16),
            pltpu.VMEM((3 * DH, blk), F32),
            pltpu.VMEM((n_seq, 8, 128), F32),
            pltpu.VMEM((n_t, 8, 128), F32),
            dma((2 * LOAD_CHUNKS + 1,)),
            dma((z,)), dma((z,)),
            dma((z, 3)), dma((z, 3)),
            dma((z,)), dma((z,)),
            dma((z,)), dma((z,)),
            dma((z,)), dma((z,)),
            dma((nc,)), dma((nc,)),
            dma((nc - 1,)), dma((nc - 1,)),
            dma((z,)), dma((z,)),
            dma((n_t - 1,)), dma((n_t - 1,)),
        ],
        compiler_params=pltpu.CompilerParams(
            collective_id=0, has_side_effects=True, vmem_limit_bytes=48 * 1024 * 1024
        ),
    )(layer_inputs, w_t, w_b, result_sensitivity, rate, events)
    weight_grad = weight_t.reshape(3, DH, blk).transpose(2, 0, 1)
    return input_t.T, weight_grad


def solution(mesh):
    return jax.shard_map(
        functools.partial(body, mesh.shape["seq"], mesh.shape["tensor"]),
        mesh=mesh,
        in_specs=(P("seq", None), P(None, None, "tensor"), P("seq", "tensor"), P("tensor"), P()),
        out_specs=(P("tensor", "seq"), P("seq", None, "tensor")),
        check_vma=False,
    )
```

time: 210 us -> 47 us (0.22)
  blocking collectives: 81.8 us -> 0 us
  waiting for transfers between devices: 74.8 us -> 0 us
  Pallas kernels: 0 us -> 40.7 us
  matrix products: 23 us -> 0 us
  between operations: 16.4 us -> 1.3 us
  other arithmetic: 9.12 us -> 0 us
    reduce_scatter x2 -> x0, waiting for transfers between devices: 74.7 us -> none  [the longest x1 60.3 us: body(): lax.psum_scatter(jnp.einsum('tr,pte->rpe', piece, grads, preferred_elemen...]
    psum x1 -> x0, blocking collectives: 40.9 us -> none  [body(): square = lax.psum(jnp.sum(summed * summed), ('seq', 'tensor'))]
    pallas_call x0 -> x1, Pallas kernels: none -> 40.7 us  [body(): pl.pallas_call(functools.partial(kernel, n_seq, n_t, entries, aligned), o...]
    all_gather x2 -> x0, blocking collectives: 30 us -> none  [the longest x1 16.7 us: body(): lax.all_gather(rev_state[None].astype(jnp.bfloat16), 'seq', axis=0, tiled...]
    dot_general x15 -> x0, matrix products: 23 us -> none  [the longest x1 4.54 us: body(): jnp.einsum('tr,pte->rpe', piece, grads, preferred_element_type=jnp.float32)]
    unnamed x1 -> x0, blocking collectives: 10.8 us -> none
    convert_element_type x3 -> x0, other arithmetic: 4.03 us -> none  [the longest x1 2.22 us: body(): (summed * factor).astype(jnp.bfloat16)]
    reduce_sum x2 -> x0, other arithmetic: 3.17 us -> none  [the longest x1 2.23 us: body(): square = lax.psum(jnp.sum(summed * summed), ('seq', 'tensor'))]
  transfers between devices with their start and end apart: 2 -> 0, of which waited for: 2 -> 0; matrix products, arithmetic and copies ran while one was open for 3% -> 0% of each run, Pallas kernels for 0% -> 0%
where the time goes in v1:
time: 47 us; the launch traced here: 46.8 us
  Pallas kernels  40.7 us (87%)
  local copies, waits for them, and re-layouts  4.74 us (10%)
  between operations  1.3 us (3%)
    pallas_call x1, Pallas kernels, body(): pl.pallas_call(functools.partial(kernel, n_seq, n_t, entries, aligned), o...  40.7 us
    unnamed x8, local copies, waits for them, and re-layouts  4.74 us

profile of v1, /device:TPU:0, one launch (start us, length us, event | category | flops | bytes accessed | tf_op | source)
XLA Modules:
  0.0 46.8 jit_solution(10731321075892774637)
XLA Ops:
  1.3 0.0 copy-start
  1.3 1.7 %copy-done = bf16[192,6144]{1,0:T(8,128)(2,1)S(1)} copy-done((bf16[192,6144]{1,0:T(8,128)(2,1)S(1)}, bf16[192,6144]{1,0:T(8,128)(2,1)}, u32[]{:S(2)}) %copy-start) | copy-done | bytes 2359320
  3.0 0.0 copy-start.1
  3.0 0.8 %copy-done.1 = bf16[192,96]{1,0:T(8,128)(2,1)S(1)} copy-done((bf16[192,96]{1,0:T(8,128)(2,1)S(1)}, bf16[192,96]{1,0:T(8,128)(2,1)}, u32[]{:S(2)}) %copy-start.1) | copy-done | bytes 36888
  3.8 0.0 copy-start.2
  3.8 0.7 %copy-done.2 = s32[4]{0:T(128)S(1)} copy-done((s32[4]{0:T(128)S(1)}, s32[4]{0:T(128)}, u32[]{:S(2)}) %copy-start.2) | copy-done | bytes 40
  4.4 40.7 %shard_map.68 = (bf16[192,768]{1,0:T(8,128)(2,1)S(1)}, bf16[288,1536]{1,0:T(8,128)(2,1)S(1)}) custom-call(bf16[192,6144]{1,0:T(8,128)(2,1)S(1)} %copy-done, bf16[288,6144]{1,0:T(8,128)(2,1)} %bitcast.9, bf16[1,8,128]{2,1,0:T(8,128)(2,1)S(1)} %broadcast_in_dim.3.wb_hbm, bf16[192,96]{1,0:T(8,128)(2,1)S(1)} %copy-done.1, f32[1]{0:T(128)S(6)} %copy.9.rate_ref, ...), custom_call_target="tpu_custom_call" | custom-call | tf_op jit(solution)/shard_map/pallas_call | solution.py:300
  45.1 0.7 %copy.10 = bf16[768,192]{0,1:T(8,128)(2,1)} copy(bf16[768,192]{0,1:T(8,128)(2,1)S(1)} %bitcast.8) | data formatting | bytes 589824
  45.9 0.9 %copy.11 = bf16[1536,3,96]{0,2,1:T(8,128)(2,1)} copy(bf16[1536,3,96]{0,2,1:T(8,128)(2,1)S(1)} %bitcast.7) | data formatting | bytes 1769472
  (1 shorter events, 0.0 us)
Async XLA Ops:
  1.3 1.7 %copy-start = (bf16[192,6144]{1,0:T(8,128)(2,1)S(1)}, bf16[192,6144]{1,0:T(8,128)(2,1)}, u32[]{:S(2)}) copy-start(bf16[192,6144]{1,0:T(8,128)(2,1)} %x_hbm.1) | copy-start | bytes 7077892
  3.0 0.8 %copy-start.1 = (bf16[192,96]{1,0:T(8,128)(2,1)S(1)}, bf16[192,96]{1,0:T(8,128)(2,1)}, u32[]{:S(2)}) copy-start(bf16[192,96]{1,0:T(8,128)(2,1)} %o_ref.1) | copy-start | bytes 110596
  3.8 0.7 %copy-start.2 = (s32[4]{0:T(128)S(1)}, s32[4]{0:T(128)}, u32[]{:S(2)}) copy-start(s32[4]{0:T(128)} %events_ref.1) | copy-start | bytes 52

commit v2 on v1

--- a/solution.py
+++ b/solution.py
@@ -26,11 +26,12 @@
 
 
 def kernel(
-    n_seq, n_t, entries, aligned,
-    x_hbm, w_hbm, wb_hbm, o_ref, rate_ref, events_ref,
+    n_seq, n_t, entries, aligned, flat,
+    x_hbm, w_hbm, wb_hbm, o_hbm, rate_hbm, events_hbm,
     ig_ref, wg_ref,
-    x, w, wb, xg, g, gt, st, ps, rc, sd, rd, acc, sqz, sqt,
-    load_sem, bx1s, bx1r, bx2s, bx2r, bx3s, bx3r, sts, str_, gs, gr,
+    x, w, wb, o_ref, rate_ref, events_ref,
+    xg, g, gx, gt, st, ps, rc, sd, rd, acc, sqz, sqt,
+    load_sem, small_sem, bx1s, bx1r, bx2s, bx2r, bx3s, bx3r, sts, str_, gs, gr,
     pss, psr, rds, rdr, zs, zr, ts, tr,
 ):
     rows, width = x_hbm.shape
@@ -56,6 +57,11 @@
             copy = pltpu.make_async_copy(src.at[:, cols], dst.at[:, cols], load_sem.at[2 * i + n])
             copy.start()
             loads.append(copy)
+    smalls = []
+    for n, (src, dst) in enumerate(((o_hbm, o_ref), (rate_hbm, rate_ref), (events_hbm, events_ref))):
+        copy = pltpu.make_async_copy(src, dst, small_sem.at[n])
+        copy.start()
+        smalls.append(copy)
     if not aligned:
         wb_copy = pltpu.make_async_copy(wb_hbm, wb, load_sem.at[2 * LOAD_CHUNKS])
         wb_copy.start()
@@ -66,12 +72,11 @@
     def t_peer(d):
         return lax.rem(j + d, n_t)
 
+    offsets = [(a, b) for a in range(n_seq) for b in range(n_t) if (flat or a * b == 0) and a + b]
     barrier = pltpu.get_barrier_semaphore()
-    for d in range(1, n_seq):
-        pl.semaphore_signal(barrier, inc=1, device_id=(seq_peer(d), j), device_id_type=MESH)
-    for d in range(1, n_t):
-        pl.semaphore_signal(barrier, inc=1, device_id=(s, t_peer(d)), device_id_type=MESH)
-    pl.semaphore_wait(barrier, n_seq + n_t - 2)
+    for a, b in offsets:
+        pl.semaphore_signal(barrier, inc=1, device_id=(seq_peer(a), t_peer(b)), device_id_type=MESH)
+    pl.semaphore_wait(barrier, len(offsets))
 
     sends = []
 
@@ -115,6 +120,8 @@
     q_t = (proj[:DH] * scale).astype(BF16)
     k_t = proj[DH : 2 * DH].astype(BF16)
     v_t = proj[2 * DH :].astype(BF16)
+    for copy in smalls:
+        copy.wait()
     o = o_ref[...]
     o_t = o.astype(F32).T.astype(BF16)
     q_r = q_t.astype(F32).T.astype(BF16)
@@ -187,8 +194,12 @@
     grads_t = jnp.concatenate([dq_t * scale, dk_t, dv_t], axis=0)
     gt[0] = grads_t.astype(BF16)
     g[...] = grads_t.T.astype(BF16)
-    for d in range(1, n_seq):
-        send(gt.at[0], gt.at[d], gs.at[d - 1], gr.at[d - 1], (seq_peer(d), j))
+    head, tail = 128, rows - 128
+    low, high = grads_t[: 3 * DH // 2, head:], grads_t[3 * DH // 2 :, head:]
+    gx[0, : 3 * DH] = grads_t[:, :head].astype(BF16)
+    gx[0, 3 * DH :] = jnp.concatenate([low, high], axis=1).astype(BF16)
+    for d in range(1, n_seq):
+        send(gx.at[0], gx.at[d], gs.at[d - 1], gr.at[d - 1], (seq_peer(d), j))
 
     step = 256 if iblk % 256 == 0 else iblk
     if not aligned:
@@ -211,14 +222,6 @@
         block_term(2 * to_chip + 1 - k, put)
         send(ps.at[m - 1], rc.at[m - 1], pss.at[m - 1], psr.at[m - 1], (s, sibling))
 
-    for d in range(1, n_seq):
-        for m in range(1, 4):
-            wait_recv(
-                piece(d, k, lax.rem(c + 4 - m, 4)),
-                bx2s.at[d - 1, m - 1], bx2r.at[d - 1, m - 1], (s, j),
-            )
-        send(token_half(d, k), token_half(d, k), bx3s.at[d - 1], bx3r.at[d - 1], (s, sibling))
-
     for m in range(1, nc):
         wait_recv(rc.at[m - 1], pss.at[m - 1], psr.at[m - 1], (s, sibling))
         to_chip = lax.rem(chip + m, nc)
@@ -227,10 +230,22 @@
         block_term(2 * to_chip + k, put)
         send(sd.at[m - 1], rd.at[m - 1], rds.at[m - 1], rdr.at[m - 1], (s, 2 * to_chip + k))
 
+    for d in range(1, n_seq):
+        for m in range(1, 4):
+            wait_recv(
+                piece(d, k, lax.rem(c + 4 - m, 4)),
+                bx2s.at[d - 1, m - 1], bx2r.at[d - 1, m - 1], (s, j),
+            )
+        send(token_half(d, k), token_half(d, k), bx3s.at[d - 1], bx3r.at[d - 1], (s, sibling))
+
     wstep = 256
     for d in range(1, n_seq):
         wait_recv(token_half(d, 1 - k), bx3s.at[d - 1], bx3r.at[d - 1], (s, sibling))
-        wait_recv(gt.at[d], gs.at[d - 1], gr.at[d - 1], (s, j))
+        wait_recv(gx.at[d], gs.at[d - 1], gr.at[d - 1], (s, j))
+        gt[d, :, :head] = gx[d, : 3 * DH]
+        packed = gx[d, 3 * DH :].astype(F32)
+        gt[d, : 3 * DH // 2, head:] = packed[:, :tail].astype(BF16)
+        gt[d, 3 * DH // 2 :, head:] = packed[:, tail:].astype(BF16)
 
     def grad_cols(i, square):
         cols = pl.ds(pl.multiple_of(i * wstep, 128), wstep)
@@ -241,9 +256,15 @@
         return square + jnp.sum((total * total).reshape(3 * DH // 8, 8, wstep), axis=0)
 
     square = lax.fori_loop(0, blk // wstep, grad_cols, jnp.zeros((8, wstep), F32))
-    sqz[0] = square[:, :128] + square[:, 128:]
-    for d in range(1, n_seq):
-        send(sqz.at[0], sqz.at[d], zs.at[d - 1], zr.at[d - 1], (seq_peer(d), j))
+    sqt[0] = square[:, :128] + square[:, 128:]
+    if flat:
+        for i, (a, b) in enumerate(offsets):
+            to = (seq_peer(a), t_peer(b))
+            send(sqt.at[0], sqt.at[i + 1], ts.at[i], tr.at[i], to)
+    else:
+        sqz[0] = sqt[0]
+        for d in range(1, n_seq):
+            send(sqz.at[0], sqz.at[d], zs.at[d - 1], zr.at[d - 1], (seq_peer(d), j))
 
     wait_recv(rc.at[nc - 1], pss.at[nc - 1], psr.at[nc - 1], (s, sibling))
     for m in range(1, nc):
@@ -255,20 +276,25 @@
             total = total + rd[m - 1, :, cols].astype(F32)
         ig_ref[:, cols] = total.astype(BF16)
 
-    for d in range(1, n_seq):
-        wait_recv(sqz.at[d], zs.at[d - 1], zr.at[d - 1], (s, j))
-    total = sqz[0]
-    for d in range(1, n_seq):
-        total = total + sqz[d]
-    sqt[0] = total
-    for d in range(1, n_t):
-        send(sqt.at[0], sqt.at[d], ts.at[d - 1], tr.at[d - 1], (s, t_peer(d)))
-    block_term(j, put)
-    for d in range(1, n_t):
-        wait_recv(sqt.at[d], ts.at[d - 1], tr.at[d - 1], (s, j))
+    if flat:
+        block_term(j, put)
+        peers = len(offsets)
+    else:
+        for d in range(1, n_seq):
+            wait_recv(sqz.at[d], zs.at[d - 1], zr.at[d - 1], (s, j))
+        total = sqz[0]
+        for d in range(1, n_seq):
+            total = total + sqz[d]
+        sqt[0] = total
+        for d in range(1, n_t):
+            send(sqt.at[0], sqt.at[d], ts.at[d - 1], tr.at[d - 1], (s, t_peer(d)))
+        block_term(j, put)
+        peers = n_t - 1
+    for i in range(peers):
+        wait_recv(sqt.at[i + 1], ts.at[i], tr.at[i], (s, j))
     total = sqt[0]
-    for d in range(1, n_t):
-        total = total + sqt[d]
+    for i in range(peers):
+        total = total + sqt[i + 1]
     total = jnp.sum(jnp.sum(total, axis=1, keepdims=True), axis=0, keepdims=True)
     factor = jnp.minimum(1.0, CLIP_RMS * math.sqrt(entries) / jnp.sqrt(total + 1e-06))
 
@@ -292,25 +318,30 @@
     else:
         w_b = w_t.reshape(3 * DH, n_t, iblk).transpose(1, 0, 2)
     entries = width * 3 * DH * n_t
+    flat = n_seq * n_t <= 64
+    peers = n_seq * n_t - 1 if flat else n_t - 1
     dma = pltpu.SemaphoreType.DMA
     anywhere = pl.BlockSpec(memory_space=pl.ANY)
     vmem = pl.BlockSpec(memory_space=pltpu.VMEM)
-    smem = pl.BlockSpec(memory_space=pltpu.SMEM)
     z = n_seq - 1
     input_t, weight_t = pl.pallas_call(
-        functools.partial(kernel, n_seq, n_t, entries, aligned),
+        functools.partial(kernel, n_seq, n_t, entries, aligned, flat),
         out_shape=(
             jax.ShapeDtypeStruct((rows, iblk), BF16),
             jax.ShapeDtypeStruct((3 * DH, blk), BF16),
         ),
-        in_specs=[anywhere, anywhere, anywhere, vmem, smem, smem],
+        in_specs=[anywhere] * 6,
         out_specs=(vmem, vmem),
         scratch_shapes=[
             pltpu.VMEM((rows, width), BF16),
             pltpu.VMEM((3 * DH, width), BF16),
             pltpu.VMEM(w_b.shape, BF16),
+            pltpu.VMEM(result_sensitivity.shape, BF16),
+            pltpu.SMEM(rate.shape, F32),
+            pltpu.SMEM(events.shape, jnp.int32),
             pltpu.VMEM((z, rows, blk), BF16),
             pltpu.VMEM((rows, 3 * DH), BF16),
+            pltpu.VMEM((n_seq, 9 * DH // 2, 128), BF16),
             pltpu.VMEM((n_seq, 3 * DH, rows), BF16),
             pltpu.VMEM((2, n_seq, DH, DH), BF16),
             pltpu.VMEM((nc, rows, iblk), BF16),
@@ -319,8 +350,8 @@
             pltpu.VMEM((nc - 1, rows, iblk), BF16),
             pltpu.VMEM((3 * DH, blk), F32),
             pltpu.VMEM((n_seq, 8, 128), F32),
-            pltpu.VMEM((n_t, 8, 128), F32),
-            dma((2 * LOAD_CHUNKS + 1,)),
+            pltpu.VMEM((peers + 1, 8, 128), F32),
+            dma((2 * LOAD_CHUNKS + 1,)), dma((3,)),
             dma((z,)), dma((z,)),
             dma((z, 3)), dma((z, 3)),
             dma((z,)), dma((z,)),
@@ -329,10 +360,10 @@
             dma((nc,)), dma((nc,)),
             dma((nc - 1,)), dma((nc - 1,)),
             dma((z,)), dma((z,)),
-            dma((n_t - 1,)), dma((n_t - 1,)),
+            dma((peers,)), dma((peers,)),
         ],
         compiler_params=pltpu.CompilerParams(
-            collective_id=0, has_side_effects=True, vmem_limit_bytes=48 * 1024 * 1024
+            collective_id=0, has_side_effects=True, vmem_limit_bytes=60 * 1024 * 1024
         ),
     )(layer_inputs, w_t, w_b, result_sensitivity, rate, events)
     weight_grad = weight_t.reshape(3, DH, blk).transpose(2, 0, 1)

time: 47 us -> 44.9 us (0.955)
  Pallas kernels: 40.7 us -> 39 us
    pallas_call x1, Pallas kernels: 40.7 us -> 39 us  [body(): pl.pallas_call(functools.partial(kernel, n_seq, n_t, entries, aligned, fl...]
    unnamed x8 -> x2, local copies, waits for them, and re-layouts: 4.74 us -> 3.83 us
    broadcast_in_dim x1, local copies, waits for them, and re-layouts: 0.01 us -> 0.58 us  [body(): w_b = jnp.zeros((1, 8, 128), BF16)]
where the time goes in v2:
time: 44.9 us; the launch traced here: 44.7 us
  Pallas kernels  39 us (87%)
  local copies, waits for them, and re-layouts  4.41 us (10%)
  between operations  1.29 us (3%)
    pallas_call x1, Pallas kernels, body(): pl.pallas_call(functools.partial(kernel, n_seq, n_t, entries, aligned, fl...  39 us
    unnamed x2, local copies, waits for them, and re-layouts  3.83 us

profile of v2, /device:TPU:0, one launch (start us, length us, event | category | flops | bytes accessed | tf_op | source)
XLA Modules:
  0.0 44.7 jit_solution(5485831213406333995)
XLA Ops:
  1.3 0.6 %broadcast_in_dim.3.wb_hbm = bf16[1,8,128]{2,1,0:T(8,128)(2,1)} broadcast(bf16[]{:T(256)} %constant.0.clone.1), dimensions={} | broadcast | bytes 2050 | tf_op jit(solution)/shard_map/broadcast_in_dim | solution.py:317
  1.9 39.0 %shard_map.68 = (bf16[192,768]{1,0:T(8,128)(2,1)}, bf16[288,1536]{1,0:T(8,128)(2,1)}) custom-call(bf16[192,6144]{1,0:T(8,128)(2,1)} %x_hbm.1, bf16[288,6144]{1,0:T(8,128)(2,1)} %bitcast.7, bf16[1,8,128]{2,1,0:T(8,128)(2,1)} %broadcast_in_dim.3.wb_hbm, bf16[192,96]{1,0:T(8,128)(2,1)} %o_hbm.1, f32[1]{0:T(128)S(6)} %copy.9.rate_hbm, s32[4]{0:T(128)} %events_hbm.1), custom_call_target="tpu_custom_call" | custom-call | tf_op jit(solution)/shard_map/pallas_call | solution.py:327
  40.9 1.7 %copy.10 = bf16[768,192]{0,1:T(8,128)(2,1)} copy(bf16[768,192]{0,1:T(8,128)(2,1)} %bitcast.9) | data formatting | bytes 589824
  42.5 2.1 %copy.11 = bf16[1536,3,96]{0,2,1:T(8,128)(2,1)} copy(bf16[1536,3,96]{0,2,1:T(8,128)(2,1)} %bitcast.8) | data formatting | bytes 1769472

commit v3 on v2

--- a/solution.py
+++ b/solution.py
@@ -30,8 +30,8 @@
     x_hbm, w_hbm, wb_hbm, o_hbm, rate_hbm, events_hbm,
     ig_ref, wg_ref,
     x, w, wb, o_ref, rate_ref, events_ref,
-    xg, g, gx, gt, st, ps, rc, sd, rd, acc, sqz, sqt,
-    load_sem, small_sem, bx1s, bx1r, bx2s, bx2r, bx3s, bx3r, sts, str_, gs, gr,
+    xg, g, gx, gt, st, ps, rc, sd, rt, rd, own, acc, sqz, sqt,
+    load_sem, small_sem, bx1s, bx1r, bx2s, bx2r, bx3s, bx3r, bx4s, bx4r, sts, str_, gs, gr,
     pss, psr, rds, rdr, zs, zr, ts, tr,
 ):
     rows, width = x_hbm.shape
@@ -48,6 +48,15 @@
     c = lax.rem(j, 8) // 2
     q = blk // 4
     half = rows // 2
+    order = sorted(range(1, n_seq), key=lambda d: min(d, n_seq - d))
+    first, rest = order[: max(1, n_seq // 2)], order[max(1, n_seq // 2) :]
+
+    def across(n):
+        a, b = lax.rem(n, 2), lax.rem(n // 2, 2)
+        return n + 1 - 2 * a, n + 2 - 4 * b, n + 3 - 2 * a - 4 * b
+
+    c_x, c_y, c_d = across(c)
+    dev_x, dev_y = group + 2 * c_x + k, group + 2 * c_y + k
 
     wide = width // LOAD_CHUNKS
     loads = []
@@ -101,15 +110,41 @@
             pl.ds(pl.multiple_of(chip_col * q, 128), q),
         ]
 
+    def quarter(d, chip_col, low):
+        start = pl.multiple_of(k * half + low * (half // 2), 16)
+        return xg.at[d - 1, pl.ds(start, half // 2), pl.ds(pl.multiple_of(chip_col * q, 128), q)]
+
+    def share(d):
+        wait_recv(piece(d, k, c), bx1s.at[d - 1], bx1r.at[d - 1], (s, j))
+        mine = piece(d, k, c)
+        send(mine, mine, bx2s.at[d - 1, 0], bx2r.at[d - 1, 0], (s, dev_x))
+        send(mine, mine, bx2s.at[d - 1, 1], bx2r.at[d - 1, 1], (s, dev_y))
+
+    def forward(d):
+        wait_recv(piece(d, k, c_x), bx2s.at[d - 1, 0], bx2r.at[d - 1, 0], (s, dev_x))
+        top = quarter(d, c_x, 0)
+        send(top, top, bx4s.at[d - 1, 0], bx4r.at[d - 1, 0], (s, dev_y))
+        wait_recv(piece(d, k, c_y), bx2s.at[d - 1, 1], bx2r.at[d - 1, 1], (s, dev_y))
+        bottom = quarter(d, c_y, 1)
+        send(bottom, bottom, bx4s.at[d - 1, 1], bx4r.at[d - 1, 1], (s, dev_x))
+
+    def meet(d):
+        wait_recv(quarter(d, c_d, 0), bx4s.at[d - 1, 0], bx4r.at[d - 1, 0], (s, dev_y))
+        wait_recv(quarter(d, c_d, 1), bx4s.at[d - 1, 1], bx4r.at[d - 1, 1], (s, dev_x))
+        send(token_half(d, k), token_half(d, k), bx3s.at[d - 1], bx3r.at[d - 1], (s, sibling))
+
     def token_half(d, core):
         return xg.at[d - 1, pl.ds(pl.multiple_of(core * half, 32), half), :]
 
-    for d in range(1, n_seq):
+    def exchange(d):
         src = x_hbm.at[
             pl.ds(pl.multiple_of(k * half, 32), half),
             pl.ds(pl.multiple_of(seq_peer(d) * blk + c * q, 128), q),
         ]
         send(src, piece(d, k, c), bx1s.at[d - 1], bx1r.at[d - 1], (seq_peer(d), j))
+
+    for d in first:
+        exchange(d)
 
     proj = jnp.zeros((3 * DH, rows), F32)
     for i in range(LOAD_CHUNKS):
@@ -153,12 +188,8 @@
         earlier = jnp.where(seq_peer(d) < s, 1, 0)
         send(st.at[earlier, 0], st.at[0, d], sts.at[d - 1], str_.at[d - 1], (seq_peer(d), j))
 
-    for d in range(1, n_seq):
-        wait_recv(piece(d, k, c), bx1s.at[d - 1], bx1r.at[d - 1], (s, j))
-        for m in range(1, 4):
-            to = group + 2 * lax.rem(c + m, 4) + k
-            mine = piece(d, k, c)
-            send(mine, mine, bx2s.at[d - 1, m - 1], bx2r.at[d - 1, m - 1], (s, to))
+    for d in rest:
+        exchange(d)
 
     t_idx = lax.broadcasted_iota(jnp.int32, (rows, rows), 0)
     s_idx = lax.broadcasted_iota(jnp.int32, (rows, rows), 1)
@@ -168,6 +199,8 @@
     weight = jnp.where(t_idx >= s_idx, jnp.exp(-jnp.maximum(decay, 0.0)), 0.0)
     scores = (mm(q_r, k_t) * weight).astype(BF16)
     dscores = (mm(o, v_t) * weight).astype(BF16)
+    for d in first:
+        share(d)
     dq_t = mm_nt(k_t, dscores)
     dk_t = mm(q_t, dscores)
     dv_t = mm(o_t, scores)
@@ -215,47 +248,98 @@
         else:
             put(pl.ds(0, iblk), mm(g[...], wb[owner]))
 
-    for m in range(1, nc + 1):
-        to_chip = lax.rem(chip + m, nc)
+    if nc == 4:
+        chip_x, chip_y, chip_d = across(chip)
+        chips = [chip_d, chip_x, chip_y, chip]
+    else:
+        chips = [lax.rem(chip + m, nc) for m in range(1, nc + 1)]
+    for m in range(nc):
         def put(cols, value, m=m):
-            ps[m - 1, :, cols] = value.astype(BF16)
-        block_term(2 * to_chip + 1 - k, put)
-        send(ps.at[m - 1], rc.at[m - 1], pss.at[m - 1], psr.at[m - 1], (s, sibling))
-
-    for m in range(1, nc):
-        wait_recv(rc.at[m - 1], pss.at[m - 1], psr.at[m - 1], (s, sibling))
-        to_chip = lax.rem(chip + m, nc)
-        def put(cols, value, m=m):
-            sd[m - 1, :, cols] = (value + rc[m - 1, :, cols].astype(F32)).astype(BF16)
-        block_term(2 * to_chip + k, put)
-        send(sd.at[m - 1], rd.at[m - 1], rds.at[m - 1], rdr.at[m - 1], (s, 2 * to_chip + k))
-
-    for d in range(1, n_seq):
-        for m in range(1, 4):
-            wait_recv(
-                piece(d, k, lax.rem(c + 4 - m, 4)),
-                bx2s.at[d - 1, m - 1], bx2r.at[d - 1, m - 1], (s, j),
-            )
-        send(token_half(d, k), token_half(d, k), bx3s.at[d - 1], bx3r.at[d - 1], (s, sibling))
+            ps[m, :, cols] = value.astype(BF16)
+        block_term(2 * chips[m] + 1 - k, put)
+        send(ps.at[m], rc.at[m], pss.at[m], psr.at[m], (s, sibling))
+    for d in rest:
+        share(d)
+
+    def pair_sum(m, put):
+        wait_recv(rc.at[m], pss.at[m], psr.at[m], (s, sibling))
+        def put_sum(cols, value):
+            put(cols, value + rc[m, :, cols].astype(F32))
+        block_term(2 * chips[m] + k, put_sum)
+
+    if nc == 4:
+        to_x, to_y = (s, 2 * chip_x + k), (s, 2 * chip_y + k)
+        top, bottom = pl.ds(0, half), pl.ds(half, half)
+        targets = [
+            (rt.at[0], to_x), (rt.at[1], to_y),
+            (rd.at[0, top], to_x), (rd.at[1, bottom], to_y),
+            (rd.at[0, bottom], to_x), (rd.at[1, top], to_y),
+        ]
+
+        def send_part(n):
+            send(sd.at[n], targets[n][0], rds.at[n], rdr.at[n], targets[n][1])
+
+        def wait_part(n):
+            wait_recv(targets[n][0], rds.at[n], rdr.at[n], targets[n][1])
+
+        for m, (a, b) in enumerate(((0, 1), (2, 4), (5, 3))):
+            def put(cols, value, a=a, b=b):
+                sd[a, :, cols] = value[:half].astype(BF16)
+                sd[b, :, cols] = value[half:].astype(BF16)
+            pair_sum(m, put)
+            for n in (a, b):
+                if n < 4:
+                    send_part(n)
+        for d in first:
+            forward(d)
+        for n, got in ((4, 1), (5, 0)):
+            wait_part(got)
+            sd[n] = (sd[n].astype(F32) + rt[got].astype(F32)).astype(BF16)
+            send_part(n)
+        arrivals = 2
+    else:
+        for m in range(nc - 1):
+            def put(cols, value, m=m):
+                sd[m, :, cols] = value.astype(BF16)
+            pair_sum(m, put)
+            send(sd.at[m], rd.at[m], rds.at[m], rdr.at[m], (s, 2 * chips[m] + k))
+        for d in first:
+            forward(d)
+        arrivals = nc - 1
+    for d in rest:
+        forward(d)
+    for d in order:
+        meet(d)
+
+    def put(cols, value):
+        own[:, cols] = value
+    pair_sum(nc - 1, put)
 
     wstep = 256
-    for d in range(1, n_seq):
-        wait_recv(token_half(d, 1 - k), bx3s.at[d - 1], bx3r.at[d - 1], (s, sibling))
-        wait_recv(gx.at[d], gs.at[d - 1], gr.at[d - 1], (s, j))
-        gt[d, :, :head] = gx[d, : 3 * DH]
-        packed = gx[d, 3 * DH :].astype(F32)
-        gt[d, : 3 * DH // 2, head:] = packed[:, :tail].astype(BF16)
-        gt[d, 3 * DH // 2 :, head:] = packed[:, tail:].astype(BF16)
-
-    def grad_cols(i, square):
+
+    def grad_cols(slot, is_last, i, square):
         cols = pl.ds(pl.multiple_of(i * wstep, 128), wstep)
-        total = mm(gt[0], x[:, pl.ds(pl.multiple_of(s * blk + i * wstep, 128), wstep)])
-        for d in range(1, n_seq):
-            total = total + mm(gt[d], xg[d - 1, :, cols])
+        if slot == 0:
+            acc[:, cols] = mm(gt[0], x[:, pl.ds(pl.multiple_of(s * blk + i * wstep, 128), wstep)])
+            return square
+        total = acc[:, cols] + mm(gt[slot], xg[slot - 1, :, cols])
         acc[:, cols] = total
-        return square + jnp.sum((total * total).reshape(3 * DH // 8, 8, wstep), axis=0)
-
-    square = lax.fori_loop(0, blk // wstep, grad_cols, jnp.zeros((8, wstep), F32))
+        if is_last:
+            square = square + jnp.sum((total * total).reshape(3 * DH // 8, 8, wstep), axis=0)
+        return square
+
+    square = jnp.zeros((8, wstep), F32)
+    for d in [0] + order:
+        if d:
+            wait_recv(gx.at[d], gs.at[d - 1], gr.at[d - 1], (s, j))
+            gt[d, :, :head] = gx[d, : 3 * DH]
+            packed = gx[d, 3 * DH :].astype(F32)
+            gt[d, : 3 * DH // 2, head:] = packed[:, :tail].astype(BF16)
+            gt[d, 3 * DH // 2 :, head:] = packed[:, tail:].astype(BF16)
+            wait_recv(token_half(d, 1 - k), bx3s.at[d - 1], bx3r.at[d - 1], (s, sibling))
+        square = lax.fori_loop(
+            0, blk // wstep, functools.partial(grad_cols, d, d == order[-1]), square
+        )
     sqt[0] = square[:, :128] + square[:, 128:]
     if flat:
         for i, (a, b) in enumerate(offsets):
@@ -266,18 +350,20 @@
         for d in range(1, n_seq):
             send(sqz.at[0], sqz.at[d], zs.at[d - 1], zr.at[d - 1], (seq_peer(d), j))
 
-    wait_recv(rc.at[nc - 1], pss.at[nc - 1], psr.at[nc - 1], (s, sibling))
-    for m in range(1, nc):
-        wait_recv(rd.at[m - 1], rds.at[m - 1], rdr.at[m - 1], (s, j))
-
-    def put(cols, value):
-        total = value + rc[nc - 1, :, cols].astype(F32)
-        for m in range(1, nc):
-            total = total + rd[m - 1, :, cols].astype(F32)
-        ig_ref[:, cols] = total.astype(BF16)
+    def finish():
+        if nc == 4:
+            for n in range(2, 6):
+                wait_part(n)
+        else:
+            for m in range(arrivals):
+                wait_recv(rd.at[m], rds.at[m], rdr.at[m], (s, j))
+        total = own[...]
+        for m in range(arrivals):
+            total = total + rd[m].astype(F32)
+        ig_ref[...] = total.astype(BF16)
 
     if flat:
-        block_term(j, put)
+        finish()
         peers = len(offsets)
     else:
         for d in range(1, n_seq):
@@ -288,7 +374,7 @@
         sqt[0] = total
         for d in range(1, n_t):
             send(sqt.at[0], sqt.at[d], ts.at[d - 1], tr.at[d - 1], (s, t_peer(d)))
-        block_term(j, put)
+        finish()
         peers = n_t - 1
     for i in range(peers):
         wait_recv(sqt.at[i + 1], ts.at[i], tr.at[i], (s, j))
@@ -314,28 +400,27 @@
     aligned = iblk % 128 == 0
     w_t = projection_matrices.transpose(1, 2, 0).reshape(3 * DH, width)
     if aligned:
-        w_b = jnp.zeros((1, 8, 128), BF16)
+        w_b = result_sensitivity
     else:
         w_b = w_t.reshape(3 * DH, n_t, iblk).transpose(1, 0, 2)
     entries = width * 3 * DH * n_t
     flat = n_seq * n_t <= 64
     peers = n_seq * n_t - 1 if flat else n_t - 1
     dma = pltpu.SemaphoreType.DMA
-    anywhere = pl.BlockSpec(memory_space=pl.ANY)
     vmem = pl.BlockSpec(memory_space=pltpu.VMEM)
     z = n_seq - 1
     input_t, weight_t = pl.pallas_call(
         functools.partial(kernel, n_seq, n_t, entries, aligned, flat),
         out_shape=(
-            jax.ShapeDtypeStruct((rows, iblk), BF16),
-            jax.ShapeDtypeStruct((3 * DH, blk), BF16),
+            pltpu.VMEM((rows, iblk), BF16),
+            pltpu.VMEM((3 * DH, blk), BF16),
         ),
-        in_specs=[anywhere] * 6,
+        in_specs=[pl.BlockSpec(memory_space=pltpu.HBM)] * 6,
         out_specs=(vmem, vmem),
         scratch_shapes=[
             pltpu.VMEM((rows, width), BF16),
             pltpu.VMEM((3 * DH, width), BF16),
-            pltpu.VMEM(w_b.shape, BF16),
+            pltpu.VMEM((8, 128) if aligned else w_b.shape, BF16),
             pltpu.VMEM(result_sensitivity.shape, BF16),
             pltpu.SMEM(rate.shape, F32),
             pltpu.SMEM(events.shape, jnp.int32),
@@ -346,19 +431,22 @@
             pltpu.VMEM((2, n_seq, DH, DH), BF16),
             pltpu.VMEM((nc, rows, iblk), BF16),
             pltpu.VMEM((nc, rows, iblk), BF16),
-            pltpu.VMEM((nc - 1, rows, iblk), BF16),
-            pltpu.VMEM((nc - 1, rows, iblk), BF16),
+            pltpu.VMEM((6, rows // 2, iblk) if nc == 4 else (nc - 1, rows, iblk), BF16),
+            pltpu.VMEM((2, rows // 2, iblk), BF16),
+            pltpu.VMEM((2 if nc == 4 else nc - 1, rows, iblk), BF16),
+            pltpu.VMEM((rows, iblk), F32),
             pltpu.VMEM((3 * DH, blk), F32),
             pltpu.VMEM((n_seq, 8, 128), F32),
             pltpu.VMEM((peers + 1, 8, 128), F32),
             dma((2 * LOAD_CHUNKS + 1,)), dma((3,)),
             dma((z,)), dma((z,)),
-            dma((z, 3)), dma((z, 3)),
+            dma((z, 2)), dma((z, 2)),
             dma((z,)), dma((z,)),
+            dma((z, 2)), dma((z, 2)),
             dma((z,)), dma((z,)),
             dma((z,)), dma((z,)),
             dma((nc,)), dma((nc,)),
-            dma((nc - 1,)), dma((nc - 1,)),
+            dma((6 if nc == 4 else nc - 1,)), dma((6 if nc == 4 else nc - 1,)),
             dma((z,)), dma((z,)),
             dma((peers,)), dma((peers,)),
         ],

time: 44.9 us -> 49.4 us (1.10)
  Pallas kernels: 39 us -> 46.4 us
  local copies, waits for them, and re-layouts: 4.41 us -> 1.63 us
    pallas_call x1, Pallas kernels: 39 us -> 46.4 us  [body(): pl.pallas_call(functools.partial(kernel, n_seq, n_t, entries, aligned, fl...]
    unnamed x2, local copies, waits for them, and re-layouts: 3.83 us -> 1.63 us
    broadcast_in_dim x1 -> x0, local copies, waits for them, and re-layouts: 0.58 us -> none  [body(): w_b = jnp.zeros((1, 8, 128), BF16)]
where the time goes in v3:
time: 49.4 us; the launch traced here: 49.3 us
  Pallas kernels  46.4 us (94%)
  local copies, waits for them, and re-layouts  1.63 us (3%)
  between operations  1.29 us (3%)
    pallas_call x1, Pallas kernels, body(): pl.pallas_call(functools.partial(kernel, n_seq, n_t, entries, aligned, fl...  46.4 us
    unnamed x2, local copies, waits for them, and re-layouts  1.63 us

profile of v3, /device:TPU:0, one launch (start us, length us, event | category | flops | bytes accessed | tf_op | source)
XLA Modules:
  0.0 49.3 jit_solution(14500131062640443951)
XLA Ops:
  1.3 46.4 %shard_map.68 = (bf16[192,768]{1,0:T(8,128)(2,1)S(1)}, bf16[288,1536]{1,0:T(8,128)(2,1)S(1)}) custom-call(bf16[192,6144]{1,0:T(8,128)(2,1)} %x_hbm.1, bf16[288,6144]{1,0:T(8,128)(2,1)} %bitcast.9, bf16[192,96]{1,0:T(8,128)(2,1)} %o_hbm.1, bf16[192,96]{1,0:T(8,128)(2,1)} %o_hbm.1, f32[1]{0:T(128)S(6)} %copy.11.rate_hbm, s32[4]{0:T(128)} %events_hbm.1), custom_call_target="tpu_custom_call" | custom-call | tf_op jit(solution)/shard_map/pallas_call | solution.py:412
  47.7 0.7 %copy.9 = bf16[768,192]{0,1:T(8,128)(2,1)} copy(bf16[768,192]{0,1:T(8,128)(2,1)S(1)} %bitcast.8) | data formatting | bytes 589824
  48.4 0.9 %copy.10 = bf16[1536,3,96]{0,2,1:T(8,128)(2,1)} copy(bf16[1536,3,96]{0,2,1:T(8,128)(2,1)S(1)} %bitcast.7) | data formatting | bytes 1769472

commit v4 on v3

--- a/solution.py
+++ b/solution.py
@@ -31,7 +31,7 @@
     ig_ref, wg_ref,
     x, w, wb, o_ref, rate_ref, events_ref,
     xg, g, gx, gt, st, ps, rc, sd, rt, rd, own, acc, sqz, sqt,
-    load_sem, small_sem, bx1s, bx1r, bx2s, bx2r, bx3s, bx3r, bx4s, bx4r, sts, str_, gs, gr,
+    load_sem, small_sem, bx1s, bx1r, bx2s, bx2r, bx3s, bx3r, sts, str_, gs, gr,
     pss, psr, rds, rdr, zs, zr, ts, tr,
 ):
     rows, width = x_hbm.shape
@@ -56,7 +56,7 @@
         return n + 1 - 2 * a, n + 2 - 4 * b, n + 3 - 2 * a - 4 * b
 
     c_x, c_y, c_d = across(c)
-    dev_x, dev_y = group + 2 * c_x + k, group + 2 * c_y + k
+    dev_x, dev_y, dev_d = group + 2 * c_x + k, group + 2 * c_y + k, group + 2 * c_d + k
 
     wide = width // LOAD_CHUNKS
     loads = []
@@ -110,27 +110,16 @@
             pl.ds(pl.multiple_of(chip_col * q, 128), q),
         ]
 
-    def quarter(d, chip_col, low):
-        start = pl.multiple_of(k * half + low * (half // 2), 16)
-        return xg.at[d - 1, pl.ds(start, half // 2), pl.ds(pl.multiple_of(chip_col * q, 128), q)]
-
     def share(d):
         wait_recv(piece(d, k, c), bx1s.at[d - 1], bx1r.at[d - 1], (s, j))
         mine = piece(d, k, c)
         send(mine, mine, bx2s.at[d - 1, 0], bx2r.at[d - 1, 0], (s, dev_x))
         send(mine, mine, bx2s.at[d - 1, 1], bx2r.at[d - 1, 1], (s, dev_y))
-
-    def forward(d):
-        wait_recv(piece(d, k, c_x), bx2s.at[d - 1, 0], bx2r.at[d - 1, 0], (s, dev_x))
-        top = quarter(d, c_x, 0)
-        send(top, top, bx4s.at[d - 1, 0], bx4r.at[d - 1, 0], (s, dev_y))
-        wait_recv(piece(d, k, c_y), bx2s.at[d - 1, 1], bx2r.at[d - 1, 1], (s, dev_y))
-        bottom = quarter(d, c_y, 1)
-        send(bottom, bottom, bx4s.at[d - 1, 1], bx4r.at[d - 1, 1], (s, dev_x))
+        send(mine, mine, bx2s.at[d - 1, 2], bx2r.at[d - 1, 2], (s, dev_d))
 
     def meet(d):
-        wait_recv(quarter(d, c_d, 0), bx4s.at[d - 1, 0], bx4r.at[d - 1, 0], (s, dev_y))
-        wait_recv(quarter(d, c_d, 1), bx4s.at[d - 1, 1], bx4r.at[d - 1, 1], (s, dev_x))
+        for n, (col, dev) in enumerate(((c_x, dev_x), (c_y, dev_y), (c_d, dev_d))):
+            wait_recv(piece(d, k, col), bx2s.at[d - 1, n], bx2r.at[d - 1, n], (s, dev))
         send(token_half(d, k), token_half(d, k), bx3s.at[d - 1], bx3r.at[d - 1], (s, sibling))
 
     def token_half(d, core):
@@ -143,7 +132,7 @@
         ]
         send(src, piece(d, k, c), bx1s.at[d - 1], bx1r.at[d - 1], (seq_peer(d), j))
 
-    for d in first:
+    for d in order:
         exchange(d)
 
     proj = jnp.zeros((3 * DH, rows), F32)
@@ -188,8 +177,8 @@
         earlier = jnp.where(seq_peer(d) < s, 1, 0)
         send(st.at[earlier, 0], st.at[0, d], sts.at[d - 1], str_.at[d - 1], (seq_peer(d), j))
 
-    for d in rest:
-        exchange(d)
+    for d in first:
+        share(d)
 
     t_idx = lax.broadcasted_iota(jnp.int32, (rows, rows), 0)
     s_idx = lax.broadcasted_iota(jnp.int32, (rows, rows), 1)
@@ -199,11 +188,12 @@
     weight = jnp.where(t_idx >= s_idx, jnp.exp(-jnp.maximum(decay, 0.0)), 0.0)
     scores = (mm(q_r, k_t) * weight).astype(BF16)
     dscores = (mm(o, v_t) * weight).astype(BF16)
-    for d in first:
-        share(d)
     dq_t = mm_nt(k_t, dscores)
     dk_t = mm(q_t, dscores)
     dv_t = mm(o_t, scores)
+
+    for d in rest:
+        share(d)
 
     prefix = jnp.zeros((DH, DH), F32)
     suffix = jnp.zeros((DH, DH), F32)
@@ -234,17 +224,12 @@
     for d in range(1, n_seq):
         send(gx.at[0], gx.at[d], gs.at[d - 1], gr.at[d - 1], (seq_peer(d), j))
 
-    step = 256 if iblk % 256 == 0 else iblk
     if not aligned:
         wb_copy.wait()
 
     def block_term(owner, put):
         if aligned:
-            def one(i, carry):
-                cols = pl.ds(pl.multiple_of(owner * iblk + i * step, 128), step)
-                put(pl.ds(pl.multiple_of(i * step, 128), step), mm(g[...], w[:, cols]))
-                return carry
-            lax.fori_loop(0, iblk // step, one, 0)
+            put(pl.ds(0, iblk), mm(g[...], w[:, pl.ds(pl.multiple_of(owner * iblk, 128), iblk)]))
         else:
             put(pl.ds(0, iblk), mm(g[...], wb[owner]))
 
@@ -258,8 +243,6 @@
             ps[m, :, cols] = value.astype(BF16)
         block_term(2 * chips[m] + 1 - k, put)
         send(ps.at[m], rc.at[m], pss.at[m], psr.at[m], (s, sibling))
-    for d in rest:
-        share(d)
 
     def pair_sum(m, put):
         wait_recv(rc.at[m], pss.at[m], psr.at[m], (s, sibling))
@@ -290,8 +273,6 @@
             for n in (a, b):
                 if n < 4:
                     send_part(n)
-        for d in first:
-            forward(d)
         for n, got in ((4, 1), (5, 0)):
             wait_part(got)
             sd[n] = (sd[n].astype(F32) + rt[got].astype(F32)).astype(BF16)
@@ -303,11 +284,7 @@
                 sd[m, :, cols] = value.astype(BF16)
             pair_sum(m, put)
             send(sd.at[m], rd.at[m], rds.at[m], rdr.at[m], (s, 2 * chips[m] + k))
-        for d in first:
-            forward(d)
         arrivals = nc - 1
-    for d in rest:
-        forward(d)
     for d in order:
         meet(d)
 
@@ -317,29 +294,32 @@
 
     wstep = 256
 
-    def grad_cols(slot, is_last, i, square):
-        cols = pl.ds(pl.multiple_of(i * wstep, 128), wstep)
-        if slot == 0:
-            acc[:, cols] = mm(gt[0], x[:, pl.ds(pl.multiple_of(s * blk + i * wstep, 128), wstep)])
-            return square
-        total = acc[:, cols] + mm(gt[slot], xg[slot - 1, :, cols])
+    def arrived(d):
+        wait_recv(gx.at[d], gs.at[d - 1], gr.at[d - 1], (s, j))
+        gt[d, :, :head] = gx[d, : 3 * DH]
+        packed = gx[d, 3 * DH :].astype(F32)
+        gt[d, : 3 * DH // 2, head:] = packed[:, :tail].astype(BF16)
+        gt[d, 3 * DH // 2 :, head:] = packed[:, tail:].astype(BF16)
+        wait_recv(token_half(d, 1 - k), bx3s.at[d - 1], bx3r.at[d - 1], (s, sibling))
+
+    for d in first:
+        arrived(d)
+    for i in range(blk // wstep):
+        cols = pl.ds(i * wstep, wstep)
+        total = mm(gt[0], x[:, pl.ds(pl.multiple_of(s * blk + i * wstep, 128), wstep)])
+        for d in first:
+            total = total + mm(gt[d], xg[d - 1, :, cols])
         acc[:, cols] = total
-        if is_last:
-            square = square + jnp.sum((total * total).reshape(3 * DH // 8, 8, wstep), axis=0)
-        return square
-
+    for d in rest:
+        arrived(d)
     square = jnp.zeros((8, wstep), F32)
-    for d in [0] + order:
-        if d:
-            wait_recv(gx.at[d], gs.at[d - 1], gr.at[d - 1], (s, j))
-            gt[d, :, :head] = gx[d, : 3 * DH]
-            packed = gx[d, 3 * DH :].astype(F32)
-            gt[d, : 3 * DH // 2, head:] = packed[:, :tail].astype(BF16)
-            gt[d, 3 * DH // 2 :, head:] = packed[:, tail:].astype(BF16)
-            wait_recv(token_half(d, 1 - k), bx3s.at[d - 1], bx3r.at[d - 1], (s, sibling))
-        square = lax.fori_loop(
-            0, blk // wstep, functools.partial(grad_cols, d, d == order[-1]), square
-        )
+    for i in range(blk // wstep):
+        cols = pl.ds(i * wstep, wstep)
+        total = acc[:, cols]
+        for d in rest:
+            total = total + mm(gt[d], xg[d - 1, :, cols])
+        acc[:, cols] = total
+        square = square + jnp.sum((total * total).reshape(3 * DH // 8, 8, wstep), axis=0)
     sqt[0] = square[:, :128] + square[:, 128:]
     if flat:
         for i, (a, b) in enumerate(offsets):
@@ -440,9 +420,8 @@
             pltpu.VMEM((peers + 1, 8, 128), F32),
             dma((2 * LOAD_CHUNKS + 1,)), dma((3,)),
             dma((z,)), dma((z,)),
-            dma((z, 2)), dma((z, 2)),
+            dma((z, 3)), dma((z, 3)),
             dma((z,)), dma((z,)),
-            dma((z, 2)), dma((z, 2)),
             dma((z,)), dma((z,)),
             dma((z,)), dma((z,)),
             dma((nc,)), dma((nc,)),

time: 49.4 us -> 38.3 us (0.78)
  Pallas kernels: 46.4 us -> 35.2 us
    pallas_call x1, Pallas kernels: 46.4 us -> 35.2 us  [body(): pl.pallas_call(functools.partial(kernel, n_seq, n_t, entries, aligned, fl...]
where the time goes in v4:
time: 38.3 us; the launch traced here: 38.1 us
  Pallas kernels  35.2 us (92%)
  local copies, waits for them, and re-layouts  1.63 us (4%)
  between operations  1.29 us (3%)
    pallas_call x1, Pallas kernels, body(): pl.pallas_call(functools.partial(kernel, n_seq, n_t, entries, aligned, fl...  35.2 us
    unnamed x2, local copies, waits for them, and re-layouts  1.63 us

profile of v4, /device:TPU:0, one launch (start us, length us, event | category | flops | bytes accessed | tf_op | source)
XLA Modules:
  0.0 38.1 jit_solution(7513921119325759746)
XLA Ops:
  1.3 35.2 %shard_map.68 = (bf16[192,768]{1,0:T(8,128)(2,1)S(1)}, bf16[288,1536]{1,0:T(8,128)(2,1)S(1)}) custom-call(bf16[192,6144]{1,0:T(8,128)(2,1)} %x_hbm.1, bf16[288,6144]{1,0:T(8,128)(2,1)} %bitcast.9, bf16[192,96]{1,0:T(8,128)(2,1)} %o_hbm.1, bf16[192,96]{1,0:T(8,128)(2,1)} %o_hbm.1, f32[1]{0:T(128)S(6)} %copy.11.rate_hbm, s32[4]{0:T(128)} %events_hbm.1), custom_call_target="tpu_custom_call" | custom-call | tf_op jit(solution)/shard_map/pallas_call | solution.py:392
  36.5 0.7 %copy.9 = bf16[768,192]{0,1:T(8,128)(2,1)} copy(bf16[768,192]{0,1:T(8,128)(2,1)S(1)} %bitcast.8) | data formatting | bytes 589824
  37.2 0.9 %copy.10 = bf16[1536,3,96]{0,2,1:T(8,128)(2,1)} copy(bf16[1536,3,96]{0,2,1:T(8,128)(2,1)S(1)} %bitcast.7) | data formatting | bytes 1769472

commit v5 on v4

--- a/solution.py
+++ b/solution.py
@@ -15,6 +15,7 @@
 F32 = jnp.float32
 BF16 = jnp.bfloat16
 LOAD_CHUNKS = 4
+WRITE_CHUNKS = 3
 
 
 def mm(a, b):
@@ -28,9 +29,9 @@
 def kernel(
     n_seq, n_t, entries, aligned, flat,
     x_hbm, w_hbm, wb_hbm, o_hbm, rate_hbm, events_hbm,
-    ig_ref, wg_ref,
+    ig_ref, acc, factor_ref,
     x, w, wb, o_ref, rate_ref, events_ref,
-    xg, g, gx, gt, st, ps, rc, sd, rt, rd, own, acc, sqz, sqt,
+    xg, g, gx, gt, st, ps, rc, sd, rt, rd, own, sqz, sqt,
     load_sem, small_sem, bx1s, bx1r, bx2s, bx2r, bx3s, bx3r, sts, str_, gs, gr,
     pss, psr, rds, rdr, zs, zr, ts, tr,
 ):
@@ -132,7 +133,7 @@
         ]
         send(src, piece(d, k, c), bx1s.at[d - 1], bx1r.at[d - 1], (seq_peer(d), j))
 
-    for d in order:
+    for d in first:
         exchange(d)
 
     proj = jnp.zeros((3 * DH, rows), F32)
@@ -177,8 +178,8 @@
         earlier = jnp.where(seq_peer(d) < s, 1, 0)
         send(st.at[earlier, 0], st.at[0, d], sts.at[d - 1], str_.at[d - 1], (seq_peer(d), j))
 
-    for d in first:
-        share(d)
+    for d in rest:
+        exchange(d)
 
     t_idx = lax.broadcasted_iota(jnp.int32, (rows, rows), 0)
     s_idx = lax.broadcasted_iota(jnp.int32, (rows, rows), 1)
@@ -192,7 +193,7 @@
     dk_t = mm(q_t, dscores)
     dv_t = mm(o_t, scores)
 
-    for d in rest:
+    for d in first:
         share(d)
 
     prefix = jnp.zeros((DH, DH), F32)
@@ -243,12 +244,24 @@
             ps[m, :, cols] = value.astype(BF16)
         block_term(2 * chips[m] + 1 - k, put)
         send(ps.at[m], rc.at[m], pss.at[m], psr.at[m], (s, sibling))
+    for d in rest:
+        share(d)
 
     def pair_sum(m, put):
         wait_recv(rc.at[m], pss.at[m], psr.at[m], (s, sibling))
         def put_sum(cols, value):
             put(cols, value + rc[m, :, cols].astype(F32))
         block_term(2 * chips[m] + k, put_sum)
+
+    wstep = 256
+
+    def own_work():
+        def put(cols, value):
+            own[:, cols] = value
+        pair_sum(nc - 1, put)
+        for i in range(blk // wstep):
+            cols = pl.ds(pl.multiple_of(s * blk + i * wstep, 128), wstep)
+            acc[:, pl.ds(i * wstep, wstep)] = mm(gt[0], x[:, cols])
 
     if nc == 4:
         to_x, to_y = (s, 2 * chip_x + k), (s, 2 * chip_y + k)
@@ -273,6 +286,7 @@
             for n in (a, b):
                 if n < 4:
                     send_part(n)
+        own_work()
         for n, got in ((4, 1), (5, 0)):
             wait_part(got)
             sd[n] = (sd[n].astype(F32) + rt[got].astype(F32)).astype(BF16)
@@ -284,15 +298,11 @@
                 sd[m, :, cols] = value.astype(BF16)
             pair_sum(m, put)
             send(sd.at[m], rd.at[m], rds.at[m], rdr.at[m], (s, 2 * chips[m] + k))
+        own_work()
         arrivals = nc - 1
     for d in order:
         meet(d)
 
-    def put(cols, value):
-        own[:, cols] = value
-    pair_sum(nc - 1, put)
-
-    wstep = 256
 
     def arrived(d):
         wait_recv(gx.at[d], gs.at[d - 1], gr.at[d - 1], (s, j))
@@ -306,7 +316,7 @@
         arrived(d)
     for i in range(blk // wstep):
         cols = pl.ds(i * wstep, wstep)
-        total = mm(gt[0], x[:, pl.ds(pl.multiple_of(s * blk + i * wstep, 128), wstep)])
+        total = acc[:, cols]
         for d in first:
             total = total + mm(gt[d], xg[d - 1, :, cols])
         acc[:, cols] = total
@@ -364,14 +374,24 @@
     total = jnp.sum(jnp.sum(total, axis=1, keepdims=True), axis=0, keepdims=True)
     factor = jnp.minimum(1.0, CLIP_RMS * math.sqrt(entries) / jnp.sqrt(total + 1e-06))
 
-    def scaled(i, carry):
-        cols = pl.ds(pl.multiple_of(i * wstep, 128), wstep)
-        wg_ref[:, cols] = (acc[:, cols] * factor).astype(BF16)
-        return carry
-
-    lax.fori_loop(0, blk // wstep, scaled, 0)
+    factor_ref[...] = jnp.broadcast_to(factor, (8, 128))
     for copy in sends:
         copy.wait_send()
+
+
+def write(input_sum, summed, factor_ref, ig_hbm, wg_hbm, scaled, sems):
+    copies = [pltpu.make_async_copy(input_sum, ig_hbm, sems.at[0])]
+    copies[0].start()
+    factor = factor_ref[:1, :1]
+    tall = summed.shape[0] // WRITE_CHUNKS
+    for i in range(WRITE_CHUNKS):
+        part = pl.ds(i * tall, tall)
+        scaled[part, :] = (summed[part, :] * factor).astype(BF16)
+        copy = pltpu.make_async_copy(scaled.at[part], wg_hbm.at[part], sems.at[i + 1])
+        copy.start()
+        copies.append(copy)
+    for copy in copies:
+        copy.wait()
 
 
 def body(n_seq, n_t, layer_inputs, projection_matrices, result_sensitivity, rate, events):
@@ -389,14 +409,15 @@
     dma = pltpu.SemaphoreType.DMA
     vmem = pl.BlockSpec(memory_space=pltpu.VMEM)
     z = n_seq - 1
-    input_t, weight_t = pl.pallas_call(
+    input_sum, summed, factor = pl.pallas_call(
         functools.partial(kernel, n_seq, n_t, entries, aligned, flat),
         out_shape=(
             pltpu.VMEM((rows, iblk), BF16),
-            pltpu.VMEM((3 * DH, blk), BF16),
+            pltpu.VMEM((3 * DH, blk), F32),
+            pltpu.VMEM((8, 128), F32),
         ),
         in_specs=[pl.BlockSpec(memory_space=pltpu.HBM)] * 6,
-        out_specs=(vmem, vmem),
+        out_specs=(vmem, vmem, vmem),
         scratch_shapes=[
             pltpu.VMEM((rows, width), BF16),
             pltpu.VMEM((3 * DH, width), BF16),
@@ -415,7 +436,6 @@
             pltpu.VMEM((2, rows // 2, iblk), BF16),
             pltpu.VMEM((2 if nc == 4 else nc - 1, rows, iblk), BF16),
             pltpu.VMEM((rows, iblk), F32),
-            pltpu.VMEM((3 * DH, blk), F32),
             pltpu.VMEM((n_seq, 8, 128), F32),
             pltpu.VMEM((peers + 1, 8, 128), F32),
             dma((2 * LOAD_CHUNKS + 1,)), dma((3,)),
@@ -430,9 +450,24 @@
             dma((peers,)), dma((peers,)),
         ],
         compiler_params=pltpu.CompilerParams(
-            collective_id=0, has_side_effects=True, vmem_limit_bytes=60 * 1024 * 1024
+            collective_id=0, has_side_effects=True, vmem_limit_bytes=56 * 1024 * 1024
         ),
     )(layer_inputs, w_t, w_b, result_sensitivity, rate, events)
+    whole = pl.BlockSpec(memory_space=pl.ANY)
+    input_t, weight_t = pl.pallas_call(
+        write,
+        out_shape=(
+            jax.ShapeDtypeStruct((rows, iblk), BF16),
+            jax.ShapeDtypeStruct((3 * DH, blk), BF16),
+        ),
+        in_specs=[vmem] * 3,
+        out_specs=(whole, whole),
+        scratch_shapes=[
+            pltpu.VMEM((3 * DH, blk), BF16),
+            dma((WRITE_CHUNKS + 1,)),
+        ],
+        compiler_params=pltpu.CompilerParams(vmem_limit_bytes=16 * 1024 * 1024),
+    )(input_sum, summed, factor)
     weight_grad = weight_t.reshape(3, DH, blk).transpose(2, 0, 1)
     return input_t.T, weight_grad
 

time: 38.3 us -> 39.2 us (1.023)
  Pallas kernels: 35.2 us -> 37.8 us
  local copies, waits for them, and re-layouts: 1.63 us -> 0 us
    unnamed x2 -> x0, local copies, waits for them, and re-layouts: 1.63 us -> none
    pallas_call x1, Pallas kernels: 35.2 us -> 36.7 us  [body(): pl.pallas_call(functools.partial(kernel, n_seq, n_t, entries, aligned, fl...]
    pallas_call x0 -> x1, Pallas kernels: none -> 1.04 us  [body(): pl.pallas_call(write, out_shape=(jax.ShapeDtypeStruct((rows, iblk), BF16)...]
where the time goes in v5:
time: 39.2 us; the launch traced here: 39.1 us
  Pallas kernels  37.8 us (96%)
  between operations  1.28 us (3%)
    pallas_call x1, Pallas kernels, body(): pl.pallas_call(functools.partial(kernel, n_seq, n_t, entries, aligned, fl...  36.7 us
    pallas_call x1, Pallas kernels, body(): pl.pallas_call(write, out_shape=(jax.ShapeDtypeStruct((rows, iblk), BF16)...  1.04 us

profile of v5, /device:TPU:0, one launch (start us, length us, event | category | flops | bytes accessed | tf_op | source)
XLA Modules:
  0.0 39.1 jit_solution(16121944345628336261)
XLA Ops:
  1.3 36.7 %shard_map.68 = (bf16[192,768]{1,0:T(8,128)(2,1)S(1)}, f32[288,1536]{1,0:T(8,128)S(1)}, f32[8,128]{1,0:T(8,128)S(1)}) custom-call(bf16[192,6144]{1,0:T(8,128)(2,1)} %x_hbm.1, bf16[288,6144]{1,0:T(8,128)(2,1)} %bitcast.7, bf16[192,96]{1,0:T(8,128)(2,1)} %o_hbm.1, bf16[192,96]{1,0:T(8,128)(2,1)} %o_hbm.1, f32[1]{0:T(128)S(6)} %copy.7.rate_hbm, s32[4]{0:T(128)} %events_hbm.1), custom_call_target="tpu_custom_call" | custom-call | tf_op jit(solution)/shard_map/pallas_call | solution.py:412
  38.0 1.0 %shard_map.69 = (bf16[192,768]{1,0:T(8,128)(2,1)}, bf16[288,1536]{1,0:T(8,128)(2,1)}) custom-call(bf16[192,768]{1,0:T(8,128)(2,1)S(1)} %get-tuple-element.7.input_sum, f32[288,1536]{1,0:T(8,128)S(1)} %get-tuple-element.8.summed, f32[8,128]{1,0:T(8,128)S(1)} %get-tuple-element.9.factor_ref), custom_call_target="tpu_custom_call" | custom-call | tf_op jit(solution)/shard_map/pallas_call | solution.py:457

commit v6 on v5

--- a/solution.py
+++ b/solution.py
@@ -114,9 +114,9 @@
     def share(d):
         wait_recv(piece(d, k, c), bx1s.at[d - 1], bx1r.at[d - 1], (s, j))
         mine = piece(d, k, c)
+        send(mine, mine, bx2s.at[d - 1, 2], bx2r.at[d - 1, 2], (s, dev_d))
         send(mine, mine, bx2s.at[d - 1, 0], bx2r.at[d - 1, 0], (s, dev_x))
         send(mine, mine, bx2s.at[d - 1, 1], bx2r.at[d - 1, 1], (s, dev_y))
-        send(mine, mine, bx2s.at[d - 1, 2], bx2r.at[d - 1, 2], (s, dev_d))
 
     def meet(d):
         for n, (col, dev) in enumerate(((c_x, dev_x), (c_y, dev_y), (c_d, dev_d))):
@@ -133,7 +133,7 @@
         ]
         send(src, piece(d, k, c), bx1s.at[d - 1], bx1r.at[d - 1], (seq_peer(d), j))
 
-    for d in first:
+    for d in order:
         exchange(d)
 
     proj = jnp.zeros((3 * DH, rows), F32)
@@ -178,8 +178,8 @@
         earlier = jnp.where(seq_peer(d) < s, 1, 0)
         send(st.at[earlier, 0], st.at[0, d], sts.at[d - 1], str_.at[d - 1], (seq_peer(d), j))
 
-    for d in rest:
-        exchange(d)
+    for d in first:
+        share(d)
 
     t_idx = lax.broadcasted_iota(jnp.int32, (rows, rows), 0)
     s_idx = lax.broadcasted_iota(jnp.int32, (rows, rows), 1)
@@ -193,7 +193,7 @@
     dk_t = mm(q_t, dscores)
     dv_t = mm(o_t, scores)
 
-    for d in first:
+    for d in rest:
         share(d)
 
     prefix = jnp.zeros((DH, DH), F32)
@@ -244,8 +244,6 @@
             ps[m, :, cols] = value.astype(BF16)
         block_term(2 * chips[m] + 1 - k, put)
         send(ps.at[m], rc.at[m], pss.at[m], psr.at[m], (s, sibling))
-    for d in rest:
-        share(d)
 
     def pair_sum(m, put):
         wait_recv(rc.at[m], pss.at[m], psr.at[m], (s, sibling))
@@ -287,6 +285,8 @@
                 if n < 4:
                     send_part(n)
         own_work()
+        for d in first:
+            meet(d)
         for n, got in ((4, 1), (5, 0)):
             wait_part(got)
             sd[n] = (sd[n].astype(F32) + rt[got].astype(F32)).astype(BF16)
@@ -299,8 +299,10 @@
             pair_sum(m, put)
             send(sd.at[m], rd.at[m], rds.at[m], rdr.at[m], (s, 2 * chips[m] + k))
         own_work()
+        for d in first:
+            meet(d)
         arrivals = nc - 1
-    for d in order:
+    for d in rest:
         meet(d)
 
 

time: 39.2 us -> 37.4 us (0.954)
  Pallas kernels: 37.8 us -> 36 us
    pallas_call x1, Pallas kernels: 36.7 us -> 35 us  [body(): pl.pallas_call(functools.partial(kernel, n_seq, n_t, entries, aligned, fl...]
where the time goes in v6:
time: 37.4 us; the launch traced here: 37.3 us
  Pallas kernels  36 us (96%)
  between operations  1.28 us (3%)
    pallas_call x1, Pallas kernels, body(): pl.pallas_call(functools.partial(kernel, n_seq, n_t, entries, aligned, fl...  35 us
    pallas_call x1, Pallas kernels, body(): pl.pallas_call(write, out_shape=(jax.ShapeDtypeStruct((rows, iblk), BF16)...  1.04 us

profile of v6, /device:TPU:0, one launch (start us, length us, event | category | flops | bytes accessed | tf_op | source)
XLA Modules:
  0.0 37.3 jit_solution(5610181840313824464)
XLA Ops:
  1.3 35.0 %shard_map.68 = (bf16[192,768]{1,0:T(8,128)(2,1)S(1)}, f32[288,1536]{1,0:T(8,128)S(1)}, f32[8,128]{1,0:T(8,128)S(1)}) custom-call(bf16[192,6144]{1,0:T(8,128)(2,1)} %x_hbm.1, bf16[288,6144]{1,0:T(8,128)(2,1)} %bitcast.7, bf16[192,96]{1,0:T(8,128)(2,1)} %o_hbm.1, bf16[192,96]{1,0:T(8,128)(2,1)} %o_hbm.1, f32[1]{0:T(128)S(6)} %copy.7.rate_hbm, s32[4]{0:T(128)} %events_hbm.1), custom_call_target="tpu_custom_call" | custom-call | tf_op jit(solution)/shard_map/pallas_call | solution.py:414
  36.2 1.0 %shard_map.69 = (bf16[192,768]{1,0:T(8,128)(2,1)}, bf16[288,1536]{1,0:T(8,128)(2,1)}) custom-call(bf16[192,768]{1,0:T(8,128)(2,1)S(1)} %get-tuple-element.7.input_sum, f32[288,1536]{1,0:T(8,128)S(1)} %get-tuple-element.8.summed, f32[8,128]{1,0:T(8,128)S(1)} %get-tuple-element.9.factor_ref), custom_call_target="tpu_custom_call" | custom-call | tf_op jit(solution)/shard_map/pallas_call | solution.py:459

commit v7 on v6

--- a/solution.py
+++ b/solution.py
@@ -57,7 +57,7 @@
         return n + 1 - 2 * a, n + 2 - 4 * b, n + 3 - 2 * a - 4 * b
 
     c_x, c_y, c_d = across(c)
-    dev_x, dev_y, dev_d = group + 2 * c_x + k, group + 2 * c_y + k, group + 2 * c_d + k
+    dev_x, dev_y = group + 2 * c_x + k, group + 2 * c_y + k
 
     wide = width // LOAD_CHUNKS
     loads = []
@@ -111,16 +111,27 @@
             pl.ds(pl.multiple_of(chip_col * q, 128), q),
         ]
 
+    def quarter(d, chip_col, low):
+        start = pl.multiple_of(k * half + low * (half // 2), 16)
+        return xg.at[d - 1, pl.ds(start, half // 2), pl.ds(pl.multiple_of(chip_col * q, 128), q)]
+
     def share(d):
         wait_recv(piece(d, k, c), bx1s.at[d - 1], bx1r.at[d - 1], (s, j))
         mine = piece(d, k, c)
-        send(mine, mine, bx2s.at[d - 1, 2], bx2r.at[d - 1, 2], (s, dev_d))
         send(mine, mine, bx2s.at[d - 1, 0], bx2r.at[d - 1, 0], (s, dev_x))
         send(mine, mine, bx2s.at[d - 1, 1], bx2r.at[d - 1, 1], (s, dev_y))
 
+    def forward(d):
+        wait_recv(piece(d, k, c_x), bx2s.at[d - 1, 0], bx2r.at[d - 1, 0], (s, dev_x))
+        top = quarter(d, c_x, 0)
+        send(top, top, bx2s.at[d - 1, 2], bx2r.at[d - 1, 2], (s, dev_y))
+        wait_recv(piece(d, k, c_y), bx2s.at[d - 1, 1], bx2r.at[d - 1, 1], (s, dev_y))
+        bottom = quarter(d, c_y, 1)
+        send(bottom, bottom, bx2s.at[d - 1, 3], bx2r.at[d - 1, 3], (s, dev_x))
+
     def meet(d):
-        for n, (col, dev) in enumerate(((c_x, dev_x), (c_y, dev_y), (c_d, dev_d))):
-            wait_recv(piece(d, k, col), bx2s.at[d - 1, n], bx2r.at[d - 1, n], (s, dev))
+        wait_recv(quarter(d, c_d, 0), bx2s.at[d - 1, 2], bx2r.at[d - 1, 2], (s, dev_y))
+        wait_recv(quarter(d, c_d, 1), bx2s.at[d - 1, 3], bx2r.at[d - 1, 3], (s, dev_x))
         send(token_half(d, k), token_half(d, k), bx3s.at[d - 1], bx3r.at[d - 1], (s, sibling))
 
     def token_half(d, core):
@@ -244,6 +255,8 @@
             ps[m, :, cols] = value.astype(BF16)
         block_term(2 * chips[m] + 1 - k, put)
         send(ps.at[m], rc.at[m], pss.at[m], psr.at[m], (s, sibling))
+    for d in first:
+        forward(d)
 
     def pair_sum(m, put):
         wait_recv(rc.at[m], pss.at[m], psr.at[m], (s, sibling))
@@ -284,6 +297,8 @@
             for n in (a, b):
                 if n < 4:
                     send_part(n)
+        for d in rest:
+            forward(d)
         own_work()
         for d in first:
             meet(d)
@@ -298,6 +313,8 @@
                 sd[m, :, cols] = value.astype(BF16)
             pair_sum(m, put)
             send(sd.at[m], rd.at[m], rds.at[m], rdr.at[m], (s, 2 * chips[m] + k))
+        for d in rest:
+            forward(d)
         own_work()
         for d in first:
             meet(d)
@@ -442,7 +459,7 @@
             pltpu.VMEM((peers + 1, 8, 128), F32),
             dma((2 * LOAD_CHUNKS + 1,)), dma((3,)),
             dma((z,)), dma((z,)),
-            dma((z, 3)), dma((z, 3)),
+            dma((z, 4)), dma((z, 4)),
             dma((z,)), dma((z,)),
             dma((z,)), dma((z,)),
             dma((z,)), dma((z,)),

time: 37.4 us -> 41.6 us (1.11)
  Pallas kernels: 36 us -> 40.2 us
    pallas_call x1, Pallas kernels: 35 us -> 39.2 us  [body(): pl.pallas_call(functools.partial(kernel, n_seq, n_t, entries, aligned, fl...]
where the time goes in v7:
time: 41.6 us; the launch traced here: 41.5 us
  Pallas kernels  40.2 us (97%)
  between operations  1.28 us (3%)
    pallas_call x1, Pallas kernels, body(): pl.pallas_call(functools.partial(kernel, n_seq, n_t, entries, aligned, fl...  39.2 us
    pallas_call x1, Pallas kernels, body(): pl.pallas_call(write, out_shape=(jax.ShapeDtypeStruct((rows, iblk), BF16)...  1.04 us

profile of v7, /device:TPU:0, one launch (start us, length us, event | category | flops | bytes accessed | tf_op | source)
XLA Modules:
  0.0 41.5 jit_solution(17427283534394190090)
XLA Ops:
  1.3 39.2 %shard_map.68 = (bf16[192,768]{1,0:T(8,128)(2,1)S(1)}, f32[288,1536]{1,0:T(8,128)S(1)}, f32[8,128]{1,0:T(8,128)S(1)}) custom-call(bf16[192,6144]{1,0:T(8,128)(2,1)} %x_hbm.1, bf16[288,6144]{1,0:T(8,128)(2,1)} %bitcast.7, bf16[192,96]{1,0:T(8,128)(2,1)} %o_hbm.1, bf16[192,96]{1,0:T(8,128)(2,1)} %o_hbm.1, f32[1]{0:T(128)S(6)} %copy.7.rate_hbm, s32[4]{0:T(128)} %events_hbm.1), custom_call_target="tpu_custom_call" | custom-call | tf_op jit(solution)/shard_map/pallas_call | solution.py:431
  40.4 1.0 %shard_map.69 = (bf16[192,768]{1,0:T(8,128)(2,1)}, bf16[288,1536]{1,0:T(8,128)(2,1)}) custom-call(bf16[192,768]{1,0:T(8,128)(2,1)S(1)} %get-tuple-element.7.input_sum, f32[288,1536]{1,0:T(8,128)S(1)} %get-tuple-element.8.summed, f32[8,128]{1,0:T(8,128)S(1)} %get-tuple-element.9.factor_ref), custom_call_target="tpu_custom_call" | custom-call | tf_op jit(solution)/shard_map/pallas_call | solution.py:476

commit v8 on v6

--- a/solution.py
+++ b/solution.py
@@ -31,7 +31,7 @@
     x_hbm, w_hbm, wb_hbm, o_hbm, rate_hbm, events_hbm,
     ig_ref, acc, factor_ref,
     x, w, wb, o_ref, rate_ref, events_ref,
-    xg, g, gx, gt, st, ps, rc, sd, rt, rd, own, sqz, sqt,
+    xg, g, gx, gt, st, ps, rc, sd, rd, own, sqz, sqt,
     load_sem, small_sem, bx1s, bx1r, bx2s, bx2r, bx3s, bx3r, sts, str_, gs, gr,
     pss, psr, rds, rdr, zs, zr, ts, tr,
 ):
@@ -261,47 +261,14 @@
             cols = pl.ds(pl.multiple_of(s * blk + i * wstep, 128), wstep)
             acc[:, pl.ds(i * wstep, wstep)] = mm(gt[0], x[:, cols])
 
-    if nc == 4:
-        to_x, to_y = (s, 2 * chip_x + k), (s, 2 * chip_y + k)
-        top, bottom = pl.ds(0, half), pl.ds(half, half)
-        targets = [
-            (rt.at[0], to_x), (rt.at[1], to_y),
-            (rd.at[0, top], to_x), (rd.at[1, bottom], to_y),
-            (rd.at[0, bottom], to_x), (rd.at[1, top], to_y),
-        ]
-
-        def send_part(n):
-            send(sd.at[n], targets[n][0], rds.at[n], rdr.at[n], targets[n][1])
-
-        def wait_part(n):
-            wait_recv(targets[n][0], rds.at[n], rdr.at[n], targets[n][1])
-
-        for m, (a, b) in enumerate(((0, 1), (2, 4), (5, 3))):
-            def put(cols, value, a=a, b=b):
-                sd[a, :, cols] = value[:half].astype(BF16)
-                sd[b, :, cols] = value[half:].astype(BF16)
-            pair_sum(m, put)
-            for n in (a, b):
-                if n < 4:
-                    send_part(n)
-        own_work()
-        for d in first:
-            meet(d)
-        for n, got in ((4, 1), (5, 0)):
-            wait_part(got)
-            sd[n] = (sd[n].astype(F32) + rt[got].astype(F32)).astype(BF16)
-            send_part(n)
-        arrivals = 2
-    else:
-        for m in range(nc - 1):
-            def put(cols, value, m=m):
-                sd[m, :, cols] = value.astype(BF16)
-            pair_sum(m, put)
-            send(sd.at[m], rd.at[m], rds.at[m], rdr.at[m], (s, 2 * chips[m] + k))
-        own_work()
-        for d in first:
-            meet(d)
-        arrivals = nc - 1
+    for m in range(nc - 1):
+        def put(cols, value, m=m):
+            sd[m, :, cols] = value.astype(BF16)
+        pair_sum(m, put)
+        send(sd.at[m], rd.at[m], rds.at[m], rdr.at[m], (s, 2 * chips[m] + k))
+    own_work()
+    for d in first:
+        meet(d)
     for d in rest:
         meet(d)
 
@@ -343,14 +310,10 @@
             send(sqz.at[0], sqz.at[d], zs.at[d - 1], zr.at[d - 1], (seq_peer(d), j))
 
     def finish():
-        if nc == 4:
-            for n in range(2, 6):
-                wait_part(n)
-        else:
-            for m in range(arrivals):
-                wait_recv(rd.at[m], rds.at[m], rdr.at[m], (s, j))
+        for m in range(nc - 1):
+            wait_recv(rd.at[m], rds.at[m], rdr.at[m], (s, j))
         total = own[...]
-        for m in range(arrivals):
+        for m in range(nc - 1):
             total = total + rd[m].astype(F32)
         ig_ref[...] = total.astype(BF16)
 
@@ -434,9 +397,8 @@
             pltpu.VMEM((2, n_seq, DH, DH), BF16),
             pltpu.VMEM((nc, rows, iblk), BF16),
             pltpu.VMEM((nc, rows, iblk), BF16),
-            pltpu.VMEM((6, rows // 2, iblk) if nc == 4 else (nc - 1, rows, iblk), BF16),
-            pltpu.VMEM((2, rows // 2, iblk), BF16),
-            pltpu.VMEM((2 if nc == 4 else nc - 1, rows, iblk), BF16),
+            pltpu.VMEM((nc - 1, rows, iblk), BF16),
+            pltpu.VMEM((nc - 1, rows, iblk), BF16),
             pltpu.VMEM((rows, iblk), F32),
             pltpu.VMEM((n_seq, 8, 128), F32),
             pltpu.VMEM((peers + 1, 8, 128), F32),
@@ -447,7 +409,7 @@
             dma((z,)), dma((z,)),
             dma((z,)), dma((z,)),
             dma((nc,)), dma((nc,)),
-            dma((6 if nc == 4 else nc - 1,)), dma((6 if nc == 4 else nc - 1,)),
+            dma((nc - 1,)), dma((nc - 1,)),
             dma((z,)), dma((z,)),
             dma((peers,)), dma((peers,)),
         ],

time: 37.4 us -> 39.2 us (1.048)
  Pallas kernels: 36 us -> 37.7 us
    pallas_call x1, Pallas kernels: 35 us -> 36.7 us  [body(): pl.pallas_call(functools.partial(kernel, n_seq, n_t, entries, aligned, fl...]
where the time goes in v8:
time: 39.2 us; the launch traced here: 39 us
  Pallas kernels  37.7 us (96%)
  between operations  1.28 us (3%)
    pallas_call x1, Pallas kernels, body(): pl.pallas_call(functools.partial(kernel, n_seq, n_t, entries, aligned, fl...  36.7 us
    pallas_call x1, Pallas kernels, body(): pl.pallas_call(write, out_shape=(jax.ShapeDtypeStruct((rows, iblk), BF16)...  1.04 us

profile of v8, /device:TPU:0, one launch (start us, length us, event | category | flops | bytes accessed | tf_op | source)
XLA Modules:
  0.0 39.0 jit_solution(5861533362367154019)
XLA Ops:
  1.3 36.7 %shard_map.68 = (bf16[192,768]{1,0:T(8,128)(2,1)S(1)}, f32[288,1536]{1,0:T(8,128)S(1)}, f32[8,128]{1,0:T(8,128)S(1)}) custom-call(bf16[192,6144]{1,0:T(8,128)(2,1)} %x_hbm.1, bf16[288,6144]{1,0:T(8,128)(2,1)} %bitcast.7, bf16[192,96]{1,0:T(8,128)(2,1)} %o_hbm.1, bf16[192,96]{1,0:T(8,128)(2,1)} %o_hbm.1, f32[1]{0:T(128)S(6)} %copy.7.rate_hbm, s32[4]{0:T(128)} %events_hbm.1), custom_call_target="tpu_custom_call" | custom-call | tf_op jit(solution)/shard_map/pallas_call | solution.py:377
  38.0 1.0 %shard_map.69 = (bf16[192,768]{1,0:T(8,128)(2,1)}, bf16[288,1536]{1,0:T(8,128)(2,1)}) custom-call(bf16[192,768]{1,0:T(8,128)(2,1)S(1)} %get-tuple-element.7.input_sum, f32[288,1536]{1,0:T(8,128)S(1)} %get-tuple-element.8.summed, f32[8,128]{1,0:T(8,128)S(1)} %get-tuple-element.9.factor_ref), custom_call_target="tpu_custom_call" | custom-call | tf_op jit(solution)/shard_map/pallas_call | solution.py:421
